TPU v7x, 32 devices: a whole 2x2x4 slice. The times are simulated.
32 devices in a mesh: tri: 32 (over z, y, x, core).
Axes of the slice: x: 2, y: 2, z: 4, core: 2. Of those that a mesh axis runs over, the one named last changes fastest.
Arguments:
- matrix_tiles: bfloat16 [512, 12, 128, 128], P('tri'), may hold values from -0.109375 to 0.109375
- columns: int32 [512, 12], P('tri'), may hold values from 0 to 511, as said below
- vectors: bfloat16 [16, 65536], P(None, 'tri'), may hold values from -6 to 6
- center: float32 [1], replicated, may hold values from -1 to 1
- halfwidth: float32 [1], replicated, may hold values from 1.5 to 3
Outputs:
- filtered_one: float32 [16, 65536], P(None, 'tri')
- filtered_two: float32 [16, 65536], P(None, 'tri')
Inputs may be any that keep to these rules, and one draw needn't show every extreme that they name: For block row i, columns[i, k] lies between max(0, (i // 16 - 4) * 16) and i; columns[i, 0] = i and columns[i, 1] = max(0, (i // 16 - 4) * 16); entries may repeat, and repeated tiles add.
All inputs are finite; a program needn't handle non-finite values.
Results may differ from a plain program's by a relative error of at most 0.0018.
Values may be sent and summed in bfloat16 or wider, within the bound.
No kernel may reach another device: no remote copies, remote signals or barrier semaphores. Data moves between devices by JAX's collectives and lax.ppermute only.
A program may use at most 64 MiB of HBM per device.

v0:
```python
import jax
import jax.numpy as jnp
from jax import lax
from jax.sharding import PartitionSpec as P

SPAN = 4


def passed_along(block, axis, distance):
    devices = range(lax.axis_size(axis))
    route = [(i - distance, i) for i in devices if i - distance in devices]
    return lax.ppermute(block, axis, route)


def fetch_window(blocks):
    pieces = []
    for offset in range(SPAN, 0, -1):
        pieces.append(passed_along(blocks, "tri", offset))
    pieces.append(blocks)
    return jnp.concatenate(pieces, axis=0)


def return_parts(spread, rows_blk):
    parts = [
        spread[(SPAN - offset) * rows_blk : (SPAN - offset + 1) * rows_blk]
        for offset in range(SPAN + 1)
    ]
    received = jnp.zeros_like(parts[0])
    for offset in range(1, SPAN + 1):
        received = received + passed_along(parts[offset], "tri", -offset)
    return parts[0] + received


def per_device(matrix_tiles, columns, vectors, center, halfwidth):
    rows_blk = matrix_tiles.shape[0]
    width = matrix_tiles.shape[2]
    count_vec = vectors.shape[0]
    lowest = (lax.axis_index("tri") - SPAN) * rows_blk
    slot_of = columns - lowest
    row_ids = lowest + SPAN * rows_blk + jnp.arange(rows_blk, dtype=jnp.int32)
    weight = jnp.where(columns == row_ids[:, None], 0.5, 1.0).astype(jnp.float32)
    slot_count = (SPAN + 1) * rows_blk
    flat_slots = slot_of.reshape(-1)

    def apply_local(blocks):
        window = fetch_window(blocks)
        picked = jnp.take(window, flat_slots, axis=0).reshape(rows_blk, -1, count_vec, width)
        forward = jnp.einsum(
            "rkvc,rkac->rkva", picked, matrix_tiles, preferred_element_type=jnp.float32
        )
        forward = jnp.sum(forward * weight[:, :, None, None], axis=1)
        behind = jnp.einsum(
            "rva,rkac->rkvc", blocks, matrix_tiles, preferred_element_type=jnp.float32
        )
        behind = (behind * weight[:, :, None, None]).reshape(-1, count_vec * width)
        spread = jnp.zeros((slot_count, count_vec * width), jnp.float32).at[flat_slots].add(behind)
        spread = spread.reshape(slot_count, count_vec, width)
        return forward + return_parts(spread, rows_blk)

    blocks = vectors.reshape(count_vec, rows_blk, width).transpose(1, 0, 2)
    initial = blocks.astype(jnp.float32)
    first = (apply_local(blocks) - center[0] * initial) / halfwidth[0]
    rounded = first.astype(jnp.bfloat16)
    second = 2.0 * (apply_local(rounded) - center[0] * first) / halfwidth[0] - initial
    first_out = first.transpose(1, 0, 2).reshape(count_vec, rows_blk * width)
    second_out = second.transpose(1, 0, 2).reshape(count_vec, rows_blk * width)
    return (first_out, second_out)


def solution(mesh):
    placed = (P("tri", None, None, None), P("tri", None), P(None, "tri"), P(), P())
    return jax.shard_map(
        per_device,
        mesh=mesh,
        in_specs=placed,
        out_specs=(P(None, "tri"), P(None, "tri")),
        check_vma=False,
    )
```

profile of v0, /device:TPU:17, one launch (start us, length us, event | category | flops | bytes accessed | tf_op | source)
XLA Modules:
  0.0 90.8 jit_solution(13071346757206786121)
XLA Ops:
  0.6 0.8 copy-done
  1.5 3.1 %collective-permute-start = (bf16[16,16,128]{2,1,0:T(8,128)(2,1)S(1)}, bf16[16,16,128]{2,1,0:T(8,128)(2,1)S(1)}, u32[]{:S(2)}, u32[]{:S(2)}) collective-permute-start(bf16[16,16,128]{2,1,0:T(8,128)(2,1)S(1)} %bitcast_bitcast_fusion.1), channel_id=1, source_target_pairs={{0,4},{1,5},{2,6},{3,7},{4,8},{5,9},{6,10},{7,11},{8,12},{9,13},{1... | collective-permute-start | bytes 196616 | tf_op jit(solution)/shard_map/ppermute | solution.py:12
  4.6 4.0 %collective-permute-start.1 = (bf16[16,16,128]{2,1,0:T(8,128)(2,1)S(1)}, bf16[16,16,128]{2,1,0:T(8,128)(2,1)S(1)}, u32[]{:S(2)}, u32[]{:S(2)}) collective-permute-start(bf16[16,16,128]{2,1,0:T(8,128)(2,1)S(1)} %bitcast_bitcast_fusion.1), channel_id=1, source_target_pairs={{0,3},{1,4},{2,5},{3,6},{4,7},{5,8},{6,9},{7,10},{8,11},{9,12},{10... | collective-permute-start | bytes 196616 | tf_op jit(solution)/shard_map/ppermute | solution.py:12
  8.6 3.1 %collective-permute-start.2 = (bf16[16,16,128]{2,1,0:T(8,128)(2,1)S(1)}, bf16[16,16,128]{2,1,0:T(8,128)(2,1)S(1)}, u32[]{:S(2)}, u32[]{:S(2)}) collective-permute-start(bf16[16,16,128]{2,1,0:T(8,128)(2,1)S(1)} %bitcast_bitcast_fusion.1), channel_id=1, source_target_pairs={{0,2},{1,3},{2,4},{3,5},{4,6},{5,7},{6,8},{7,9},{8,10},{9,11},{10,... | collective-permute-start | bytes 196616 | tf_op jit(solution)/shard_map/ppermute | solution.py:12
  11.8 2.8 %collective-permute-start.3 = (bf16[16,16,128]{2,1,0:T(8,128)(2,1)S(1)}, bf16[16,16,128]{2,1,0:T(8,128)(2,1)S(1)}, u32[]{:S(2)}, u32[]{:S(2)}) collective-permute-start(bf16[16,16,128]{2,1,0:T(8,128)(2,1)S(1)} %bitcast_bitcast_fusion.1), channel_id=1, source_target_pairs={{0,1},{1,2},{2,3},{3,4},{4,5},{5,6},{6,7},{7,8},{8,9},{9,10},{10,1... | collective-permute-start | bytes 196616 | tf_op jit(solution)/shard_map/ppermute | solution.py:12
  14.6 0.7 broadcast_subtract_fusion
  15.3 0.8 compare_select_fusion
  16.2 3.7 %convolution_multiply_fusion = f32[16,12,128,16]{2,3,1,0:T(8,128)S(1)} fusion(bf16[16,12,128,128]{3,2,1,0:T(8,128)(2,1)} %param.7, f32[16,12]{1,0:T(8,128)S(1)} %compare_select_fusion, bf16[16,2048]{1,0:T(8,128)(2,1)S(1)} %copy-done), kind=kOutput, calls=%fused_computation.12 | convolution fusion | flops 101056512 | bytes 7930624 | tf_op jit(solution)/shard_map/rva,rkac->rkvc/dot_general | solution.py:52
  19.9 3.6 %scatter_custom_fusion = f32[80,2048]{1,0:T(8,128)S(1)} fusion(s32[192]{0:T(256)S(1)} %bitcast.143, f32[24,8,16,128]{3,2,1,0:T(8,128)S(1)} %bitcast.136, f32[]{:T(128)} %constant.12.clone.1), kind=kCustom, calls=%fused_computation.7 | custom fusion | flops 393216 | bytes 2228228 | tf_op jit(solution)/shard_map/scatter-add | solution.py:56
  23.6 0.7 copy.17
  24.2 1.9 %collective-permute-start.4 = (f32[16,16,128]{2,1,0:T(8,128)}, f32[16,16,128]{2,1,0:T(8,128)S(1)}, u32[]{:S(2)}, u32[]{:S(2)}) collective-permute-start(f32[16,16,128]{2,1,0:T(8,128)} %bitcast.29), channel_id=1, source_target_pairs={{1,0},{2,1},{3,2},{4,3},{5,4},{6,5},{7,6},{8,7},{9,8},{10,9},{11,1... | collective-permute-start | bytes 393224 | tf_op jit(solution)/shard_map/ppermute | solution.py:12
  26.9 0.7 copy.19
  27.6 0.7 copy.20
  29.6 4.0 %collective-permute-start.5 = (f32[16,16,128]{2,1,0:T(8,128)}, f32[16,16,128]{2,1,0:T(8,128)}, u32[]{:S(2)}, u32[]{:S(2)}) collective-permute-start(f32[16,16,128]{2,1,0:T(8,128)} %bitcast.31), channel_id=1, source_target_pairs={{2,0},{3,1},{4,2},{5,3},{6,4},{7,5},{8,6},{9,7},{10,8},{11,9},{12,... | collective-permute-start | bytes 393224 | tf_op jit(solution)/shard_map/ppermute | solution.py:12
  33.6 3.9 %collective-permute-start.6 = (f32[16,16,128]{2,1,0:T(8,128)}, f32[16,16,128]{2,1,0:T(8,128)}, u32[]{:S(2)}, u32[]{:S(2)}) collective-permute-start(f32[16,16,128]{2,1,0:T(8,128)} %bitcast.33), channel_id=1, source_target_pairs={{3,0},{4,1},{5,2},{6,3},{7,4},{8,5},{9,6},{10,7},{11,8},{12,9},{13... | collective-permute-start | bytes 393224 | tf_op jit(solution)/shard_map/ppermute | solution.py:12
  37.5 3.0 %collective-permute-start.7 = (f32[16,16,128]{2,1,0:T(8,128)}, f32[16,16,128]{2,1,0:T(8,128)}, u32[]{:S(2)}, u32[]{:S(2)}) collective-permute-start(f32[16,16,128]{2,1,0:T(8,128)} %bitcast.35), channel_id=1, source_target_pairs={{4,0},{5,1},{6,2},{7,3},{8,4},{9,5},{10,6},{11,7},{12,8},{13,9},{1... | collective-permute-start | bytes 393224 | tf_op jit(solution)/shard_map/ppermute | solution.py:12
  40.7 0.8 gather_fusion
  41.7 6.3 %multiply_reduce_fusion.1 = f32[16,16,128]{2,1,0:T(8,128)S(1)} fusion(bf16[16,12,16,128]{3,2,1,0:T(8,128)(2,1)S(1)} %bitcast.138, bf16[16,12,128,128]{3,2,1,0:T(8,128)(2,1)} %param.7, f32[16,12]{1,0:T(8,128)S(1)} %compare_select_fusion), kind=kOutput, calls=%fused_computation.11 | convolution fusion | flops 101416960 | bytes 7209728 | tf_op jit(solution)/shard_map/rkvc,rkac->rkva/dot_general | solution.py:48
  48.1 1.1 %fusion.18 = (bf16[16,16,128]{2,1,0:T(8,128)(2,1)S(1)}, f32[16,16,128]{2,1,0:T(8,128)S(1)}) fusion(f32[]{:T(128)} %bitcast.131, f32[]{:T(128)} %bitcast.129, f32[16,16,128]{2,1,0:T(8,128)S(1)} %multiply_reduce_fusion.1, f32[16,16,128]{2,1,0:T(8,128)} %collective-permute-done.7, f32[16,16,128]{2,1,0:T(8,128)} %collective-permute-done.6, ...), kind=kLoop, calls=%fused_computation.63 | loop fusion | flops 327680 | bytes 1048584 | tf_op jit(solution)/shard_map/convert_element_type | solution.py:63
  49.2 2.2 %collective-permute-start.8 = (bf16[16,16,128]{2,1,0:T(8,128)(2,1)S(1)}, bf16[16,16,128]{2,1,0:T(8,128)(2,1)S(1)}, u32[]{:S(2)}, u32[]{:S(2)}) collective-permute-start(bf16[16,16,128]{2,1,0:T(8,128)(2,1)S(1)} %get-tuple-element.3), channel_id=1, source_target_pairs={{0,4},{1,5},{2,6},{3,7},{4,8},{5,9},{6,10},{7,11},{8,12},{9,13},{1... | collective-permute-start | bytes 196616 | tf_op jit(solution)/shard_map/ppermute | solution.py:12
  51.5 3.2 %collective-permute-start.9 = (bf16[16,16,128]{2,1,0:T(8,128)(2,1)S(1)}, bf16[16,16,128]{2,1,0:T(8,128)(2,1)S(1)}, u32[]{:S(2)}, u32[]{:S(2)}) collective-permute-start(bf16[16,16,128]{2,1,0:T(8,128)(2,1)S(1)} %get-tuple-element.3), channel_id=1, source_target_pairs={{0,3},{1,4},{2,5},{3,6},{4,7},{5,8},{6,9},{7,10},{8,11},{9,12},{10... | collective-permute-start | bytes 196616 | tf_op jit(solution)/shard_map/ppermute | solution.py:12
  54.7 2.5 %collective-permute-start.10 = (bf16[16,16,128]{2,1,0:T(8,128)(2,1)S(1)}, bf16[16,16,128]{2,1,0:T(8,128)(2,1)S(1)}, u32[]{:S(2)}, u32[]{:S(2)}) collective-permute-start(bf16[16,16,128]{2,1,0:T(8,128)(2,1)S(1)} %get-tuple-element.3), channel_id=1, source_target_pairs={{0,2},{1,3},{2,4},{3,5},{4,6},{5,7},{6,8},{7,9},{8,10},{9,11},{10,... | collective-permute-start | bytes 196616 | tf_op jit(solution)/shard_map/ppermute | solution.py:12
  57.2 3.6 %collective-permute-start.11 = (bf16[16,16,128]{2,1,0:T(8,128)(2,1)S(1)}, bf16[16,16,128]{2,1,0:T(8,128)(2,1)S(1)}, u32[]{:S(2)}, u32[]{:S(2)}) collective-permute-start(bf16[16,16,128]{2,1,0:T(8,128)(2,1)S(1)} %get-tuple-element.3), channel_id=1, source_target_pairs={{0,1},{1,2},{2,3},{3,4},{4,5},{5,6},{6,7},{7,8},{8,9},{9,10},{10,1... | collective-permute-start | bytes 196616 | tf_op jit(solution)/shard_map/ppermute | solution.py:12
  60.9 2.1 %convolution_multiply_fusion.1 = f32[16,16,12,128]{3,1,2,0:T(8,128)} fusion(bf16[16,12,128,128]{3,2,1,0:T(8,128)(2,1)S(1)} %bitcast.134, f32[16,12]{1,0:T(8,128)S(1)} %compare_select_fusion, bf16[16,16,128]{2,1,0:T(8,128)(2,1)S(1)} %get-tuple-element.3), kind=kOutput, calls=%fused_computation.13 | convolution fusion | flops 101056512 | bytes 7930624 | tf_op jit(solution)/shard_map/rva,rkac->rkvc/dot_general | solution.py:52
  63.0 4.5 %scatter_custom_fusion.1 = f32[80,2048]{1,0:T(8,128)S(1)} fusion(s32[192]{0:T(256)} %bitcast.144, f32[24,8,16,128]{3,2,1,0:T(8,128)} %bitcast.135, f32[]{:T(128)} %constant.12.clone.1), kind=kCustom, calls=%fused_computation.4 | custom fusion | flops 393216 | bytes 2228736 | tf_op jit(solution)/shard_map/scatter-add | solution.py:56
  67.5 2.3 %collective-permute-start.12 = (f32[16,16,128]{2,1,0:T(8,128)S(1)}, f32[16,16,128]{2,1,0:T(8,128)S(1)}, u32[]{:S(2)}, u32[]{:S(2)}) collective-permute-start(f32[16,16,128]{2,1,0:T(8,128)S(1)} %bitcast.139), channel_id=1, source_target_pairs={{1,0},{2,1},{3,2},{4,3},{5,4},{6,5},{7,6},{8,7},{9,8},{10,9},{11,1... | collective-permute-start | bytes 393224 | tf_op jit(solution)/shard_map/ppermute | solution.py:12
  70.6 5.1 %collective-permute-start.13 = (f32[16,16,128]{2,1,0:T(8,128)S(1)}, f32[16,16,128]{2,1,0:T(8,128)S(1)}, u32[]{:S(2)}, u32[]{:S(2)}) collective-permute-start(f32[16,16,128]{2,1,0:T(8,128)S(1)} %bitcast.142), channel_id=1, source_target_pairs={{2,0},{3,1},{4,2},{5,3},{6,4},{7,5},{8,6},{9,7},{10,8},{11,9},{12,... | collective-permute-start | bytes 393224 | tf_op jit(solution)/shard_map/ppermute | solution.py:12
  75.7 3.0 %collective-permute-start.14 = (f32[16,16,128]{2,1,0:T(8,128)S(1)}, f32[16,16,128]{2,1,0:T(8,128)S(1)}, u32[]{:S(2)}, u32[]{:S(2)}) collective-permute-start(f32[16,16,128]{2,1,0:T(8,128)S(1)} %bitcast.141), channel_id=1, source_target_pairs={{3,0},{4,1},{5,2},{6,3},{7,4},{8,5},{9,6},{10,7},{11,8},{12,9},{13... | collective-permute-start | bytes 393224 | tf_op jit(solution)/shard_map/ppermute | solution.py:12
  78.7 3.9 %collective-permute-start.15 = (f32[16,16,128]{2,1,0:T(8,128)S(1)}, f32[16,16,128]{2,1,0:T(8,128)S(1)}, u32[]{:S(2)}, u32[]{:S(2)}) collective-permute-start(f32[16,16,128]{2,1,0:T(8,128)S(1)} %bitcast.140), channel_id=1, source_target_pairs={{4,0},{5,1},{6,2},{7,3},{8,4},{9,5},{10,6},{11,7},{12,8},{13,9},{1... | collective-permute-start | bytes 393224 | tf_op jit(solution)/shard_map/ppermute | solution.py:12
  82.7 0.8 gather_fusion.1
  83.8 6.2 %multiply_reduce_fusion = f32[16,16,128]{2,1,0:T(8,128)S(1)} fusion(bf16[16,12,16,128]{3,2,1,0:T(8,128)(2,1)S(1)} %bitcast.137, bf16[16,12,128,128]{3,2,1,0:T(8,128)(2,1)} %param.7, f32[16,12]{1,0:T(8,128)S(1)} %compare_select_fusion), kind=kOutput, calls=%fused_computation.10 | convolution fusion | flops 101416960 | bytes 7209728 | tf_op jit(solution)/shard_map/rkvc,rkac->rkva/dot_general | solution.py:48
  90.0 0.7 copy_bitcast_fusion
  (54 shorter events, 2.6 us)
Async XLA Ops:
  0.6 0.8 copy-start
  1.5 28.1 %collective-permute-start = (bf16[16,16,128]{2,1,0:T(8,128)(2,1)S(1)}, bf16[16,16,128]{2,1,0:T(8,128)(2,1)S(1)}, u32[]{:S(2)}, u32[]{:S(2)}) collective-permute-start(bf16[16,16,128]{2,1,0:T(8,128)(2,1)S(1)} %bitcast_bitcast_fusion.1), channel_id=1, source_target_pairs={{0,4},{1,5},{2,6},{3,7},{4,8},{5,9},{6,10},{7,11},{8,12},{9,13},{1... | collective-permute-start | bytes 196616 | tf_op jit(solution)/shard_map/ppermute | solution.py:12
  4.6 29.0 %collective-permute-start.1 = (bf16[16,16,128]{2,1,0:T(8,128)(2,1)S(1)}, bf16[16,16,128]{2,1,0:T(8,128)(2,1)S(1)}, u32[]{:S(2)}, u32[]{:S(2)}) collective-permute-start(bf16[16,16,128]{2,1,0:T(8,128)(2,1)S(1)} %bitcast_bitcast_fusion.1), channel_id=1, source_target_pairs={{0,3},{1,4},{2,5},{3,6},{4,7},{5,8},{6,9},{7,10},{8,11},{9,12},{10... | collective-permute-start | bytes 196616 | tf_op jit(solution)/shard_map/ppermute | solution.py:12
  8.6 28.9 %collective-permute-start.2 = (bf16[16,16,128]{2,1,0:T(8,128)(2,1)S(1)}, bf16[16,16,128]{2,1,0:T(8,128)(2,1)S(1)}, u32[]{:S(2)}, u32[]{:S(2)}) collective-permute-start(bf16[16,16,128]{2,1,0:T(8,128)(2,1)S(1)} %bitcast_bitcast_fusion.1), channel_id=1, source_target_pairs={{0,2},{1,3},{2,4},{3,5},{4,6},{5,7},{6,8},{7,9},{8,10},{9,11},{10,... | collective-permute-start | bytes 196616 | tf_op jit(solution)/shard_map/ppermute | solution.py:12
  11.8 28.8 %collective-permute-start.3 = (bf16[16,16,128]{2,1,0:T(8,128)(2,1)S(1)}, bf16[16,16,128]{2,1,0:T(8,128)(2,1)S(1)}, u32[]{:S(2)}, u32[]{:S(2)}) collective-permute-start(bf16[16,16,128]{2,1,0:T(8,128)(2,1)S(1)} %bitcast_bitcast_fusion.1), channel_id=1, source_target_pairs={{0,1},{1,2},{2,3},{3,4},{4,5},{5,6},{6,7},{7,8},{8,9},{9,10},{10,1... | collective-permute-start | bytes 196616 | tf_op jit(solution)/shard_map/ppermute | solution.py:12
  16.2 3.7 %copy-start.1 = (s32[192,1]{0,1:T(1,128)}, s32[192,1]{0,1:T(1,128)S(1)}, u32[]{:S(2)}) copy-start(s32[192,1]{0,1:T(1,128)S(1)} %compare_select_fusion.1) | copy-start | bytes 2308
  24.2 23.8 %collective-permute-start.4 = (f32[16,16,128]{2,1,0:T(8,128)}, f32[16,16,128]{2,1,0:T(8,128)S(1)}, u32[]{:S(2)}, u32[]{:S(2)}) collective-permute-start(f32[16,16,128]{2,1,0:T(8,128)} %bitcast.29), channel_id=1, source_target_pairs={{1,0},{2,1},{3,2},{4,3},{5,4},{6,5},{7,6},{8,7},{9,8},{10,9},{11,1... | collective-permute-start | bytes 393224 | tf_op jit(solution)/shard_map/ppermute | solution.py:12
  29.6 18.5 %collective-permute-start.5 = (f32[16,16,128]{2,1,0:T(8,128)}, f32[16,16,128]{2,1,0:T(8,128)}, u32[]{:S(2)}, u32[]{:S(2)}) collective-permute-start(f32[16,16,128]{2,1,0:T(8,128)} %bitcast.31), channel_id=1, source_target_pairs={{2,0},{3,1},{4,2},{5,3},{6,4},{7,5},{8,6},{9,7},{10,8},{11,9},{12,... | collective-permute-start | bytes 393224 | tf_op jit(solution)/shard_map/ppermute | solution.py:12
  33.6 14.5 %collective-permute-start.6 = (f32[16,16,128]{2,1,0:T(8,128)}, f32[16,16,128]{2,1,0:T(8,128)}, u32[]{:S(2)}, u32[]{:S(2)}) collective-permute-start(f32[16,16,128]{2,1,0:T(8,128)} %bitcast.33), channel_id=1, source_target_pairs={{3,0},{4,1},{5,2},{6,3},{7,4},{8,5},{9,6},{10,7},{11,8},{12,9},{13... | collective-permute-start | bytes 393224 | tf_op jit(solution)/shard_map/ppermute | solution.py:12
  37.5 10.6 %collective-permute-start.7 = (f32[16,16,128]{2,1,0:T(8,128)}, f32[16,16,128]{2,1,0:T(8,128)}, u32[]{:S(2)}, u32[]{:S(2)}) collective-permute-start(f32[16,16,128]{2,1,0:T(8,128)} %bitcast.35), channel_id=1, source_target_pairs={{4,0},{5,1},{6,2},{7,3},{8,4},{9,5},{10,6},{11,7},{12,8},{13,9},{1... | collective-permute-start | bytes 393224 | tf_op jit(solution)/shard_map/ppermute | solution.py:12
  40.7 20.2 %slice-start = ((s8[6291456]{0:T(1024)(128)(4,1)}), s8[2097152]{0:T(1024)(128)(4,1)S(1)}, s32[]{:S(2)}) async-start(s8[6291456]{0:T(1024)(128)(4,1)} %bitcast.133), calls=%async_computation | async-start | bytes 4194304
  41.7 19.1 %slice-start.1 = ((s8[6291456]{0:T(1024)(128)(4,1)}), s8[4194304]{0:T(1024)(128)(4,1)S(1)}, s32[]{:S(2)}) async-start(s8[6291456]{0:T(1024)(128)(4,1)} %bitcast.133), calls=%async_computation.1 | async-start | bytes 8388608
  49.2 21.4 %collective-permute-start.8 = (bf16[16,16,128]{2,1,0:T(8,128)(2,1)S(1)}, bf16[16,16,128]{2,1,0:T(8,128)(2,1)S(1)}, u32[]{:S(2)}, u32[]{:S(2)}) collective-permute-start(bf16[16,16,128]{2,1,0:T(8,128)(2,1)S(1)} %get-tuple-element.3), channel_id=1, source_target_pairs={{0,4},{1,5},{2,6},{3,7},{4,8},{5,9},{6,10},{7,11},{8,12},{9,13},{1... | collective-permute-start | bytes 196616 | tf_op jit(solution)/shard_map/ppermute | solution.py:12
  51.5 24.2 %collective-permute-start.9 = (bf16[16,16,128]{2,1,0:T(8,128)(2,1)S(1)}, bf16[16,16,128]{2,1,0:T(8,128)(2,1)S(1)}, u32[]{:S(2)}, u32[]{:S(2)}) collective-permute-start(bf16[16,16,128]{2,1,0:T(8,128)(2,1)S(1)} %get-tuple-element.3), channel_id=1, source_target_pairs={{0,3},{1,4},{2,5},{3,6},{4,7},{5,8},{6,9},{7,10},{8,11},{9,12},{10... | collective-permute-start | bytes 196616 | tf_op jit(solution)/shard_map/ppermute | solution.py:12
  54.7 24.1 %collective-permute-start.10 = (bf16[16,16,128]{2,1,0:T(8,128)(2,1)S(1)}, bf16[16,16,128]{2,1,0:T(8,128)(2,1)S(1)}, u32[]{:S(2)}, u32[]{:S(2)}) collective-permute-start(bf16[16,16,128]{2,1,0:T(8,128)(2,1)S(1)} %get-tuple-element.3), channel_id=1, source_target_pairs={{0,2},{1,3},{2,4},{3,5},{4,6},{5,7},{6,8},{7,9},{8,10},{9,11},{10,... | collective-permute-start | bytes 196616 | tf_op jit(solution)/shard_map/ppermute | solution.py:12
  57.2 25.5 %collective-permute-start.11 = (bf16[16,16,128]{2,1,0:T(8,128)(2,1)S(1)}, bf16[16,16,128]{2,1,0:T(8,128)(2,1)S(1)}, u32[]{:S(2)}, u32[]{:S(2)}) collective-permute-start(bf16[16,16,128]{2,1,0:T(8,128)(2,1)S(1)} %get-tuple-element.3), channel_id=1, source_target_pairs={{0,1},{1,2},{2,3},{3,4},{4,5},{5,6},{6,7},{7,8},{8,9},{9,10},{10,1... | collective-permute-start | bytes 196616 | tf_op jit(solution)/shard_map/ppermute | solution.py:12
  67.5 22.5 %collective-permute-start.12 = (f32[16,16,128]{2,1,0:T(8,128)S(1)}, f32[16,16,128]{2,1,0:T(8,128)S(1)}, u32[]{:S(2)}, u32[]{:S(2)}) collective-permute-start(f32[16,16,128]{2,1,0:T(8,128)S(1)} %bitcast.139), channel_id=1, source_target_pairs={{1,0},{2,1},{3,2},{4,3},{5,4},{6,5},{7,6},{8,7},{9,8},{10,9},{11,1... | collective-permute-start | bytes 393224 | tf_op jit(solution)/shard_map/ppermute | solution.py:12
  70.6 19.4 %collective-permute-start.13 = (f32[16,16,128]{2,1,0:T(8,128)S(1)}, f32[16,16,128]{2,1,0:T(8,128)S(1)}, u32[]{:S(2)}, u32[]{:S(2)}) collective-permute-start(f32[16,16,128]{2,1,0:T(8,128)S(1)} %bitcast.142), channel_id=1, source_target_pairs={{2,0},{3,1},{4,2},{5,3},{6,4},{7,5},{8,6},{9,7},{10,8},{11,9},{12,... | collective-permute-start | bytes 393224 | tf_op jit(solution)/shard_map/ppermute | solution.py:12
  75.7 14.3 %collective-permute-start.14 = (f32[16,16,128]{2,1,0:T(8,128)S(1)}, f32[16,16,128]{2,1,0:T(8,128)S(1)}, u32[]{:S(2)}, u32[]{:S(2)}) collective-permute-start(f32[16,16,128]{2,1,0:T(8,128)S(1)} %bitcast.141), channel_id=1, source_target_pairs={{3,0},{4,1},{5,2},{6,3},{7,4},{8,5},{9,6},{10,7},{11,8},{12,9},{13... | collective-permute-start | bytes 393224 | tf_op jit(solution)/shard_map/ppermute | solution.py:12
  78.7 11.3 %collective-permute-start.15 = (f32[16,16,128]{2,1,0:T(8,128)S(1)}, f32[16,16,128]{2,1,0:T(8,128)S(1)}, u32[]{:S(2)}, u32[]{:S(2)}) collective-permute-start(f32[16,16,128]{2,1,0:T(8,128)S(1)} %bitcast.140), channel_id=1, source_target_pairs={{4,0},{5,1},{6,2},{7,3},{8,4},{9,5},{10,6},{11,7},{12,8},{13,9},{1... | collective-permute-start | bytes 393224 | tf_op jit(solution)/shard_map/ppermute | solution.py:12
where the time goes:
time: 91.5 us; the launch traced here: 90.8 us
  starting transfers between devices  51.7 us (57%)
  matrix products  18.3 us (20%)
  other arithmetic  11.9 us (13%)
  local copies, waits for them, and re-layouts  6.36 us (7%)
  between operations  2.42 us (3%)
    ppermute x16, starting transfers between devices, passed_along(): return lax.ppermute(block, axis, route)  51.7 us
    dot_general x2, matrix products, apply_local(): jnp.einsum('rkvc,rkac->rkva', picked, matrix_tiles, preferred_element_typ...  12.5 us
    scatter-add x2, other arithmetic, apply_local(): jnp.zeros((slot_count, count_vec * width), jnp.float32).at[flat_slots]  8.05 us
    dot_general x2, matrix products, apply_local(): jnp.einsum('rva,rkac->rkvc', blocks, matrix_tiles, preferred_element_type...  5.81 us
    unnamed x28, local copies, waits for them, and re-layouts  3.92 us
  transfers between devices with their start and end apart: 16, of which 0 were waited for; matrix products, arithmetic and copies ran while one was open for 37% of the time, Pallas kernels for 0%

commit v1 on v0

v1 whole, which is shorter than its diff:
```python
import jax
import jax.numpy as jnp
from jax import lax
from jax.experimental import pallas as pl
from jax.experimental.pallas import tpu as pltpu
from jax.sharding import PartitionSpec as P

SPAN = 4
MIB = 1 << 20
LANES = 128


def rotated(block, distance):
    size = lax.axis_size("tri")
    return lax.ppermute(block, "tri", [(i, (i + distance) % size) for i in range(size)])


def exchanged(block):
    return lax.ppermute(block, "tri", [(i, i ^ 1) for i in range(lax.axis_size("tri"))])


def lanes(index, width):
    return pl.ds(pl.multiple_of(index * width, width), width)


def lowest_row(cols):
    return cols[0, 0] - SPAN * cols.shape[0]


def stacked_tiles(tiles, i):
    count = tiles.shape[1]
    return jnp.concatenate(
        [jnp.concatenate([tiles[i + j, k] for k in range(count)], axis=1) for j in range(2)], axis=0
    )


def spread_rows(cols, tiles, own, spread, begin, number):
    rows, count, width, _ = tiles.shape
    vectors = own.shape[0]
    lowest = lowest_row(cols)
    for step in range(0, number, 2):
        i = begin + step
        mine = [own[:, lanes(i + j, width)] for j in range(2)]
        zero = jnp.zeros_like(mine[0])
        both = jnp.concatenate(
            [jnp.concatenate([mine[0], zero], axis=1), jnp.concatenate([zero, mine[1]], axis=1)], axis=0
        )
        product = jnp.dot(both, stacked_tiles(tiles, i), preferred_element_type=jnp.float32)
        for j in range(2):
            for k in range(count):
                column = cols[i + j, k]
                slot = column - lowest
                weight = jnp.where(column == cols[i + j, 0], 0.5, 1.0).astype(jnp.float32)
                place = lanes(lax.rem(slot, rows), width)
                part = product[j * vectors : (j + 1) * vectors, k * width : (k + 1) * width]
                spread[lax.div(slot, rows), :, place] += part * weight


def hand_over(spread, odd, even):
    odd[0] = spread[1]
    odd[1] = spread[3]
    even[0] = spread[0]
    even[1] = spread[2]
    even[2] = spread[4]


def unrolled(rows):
    assert rows % 2 == 0
    return rows if rows <= 16 else 2


def parts_loaded(rows):
    assert rows % 2 == 0
    return [4] * ((rows - 4) // 4) + [2] * ((rows - 4) % 4 // 2) + [2, 2]


def loading_kernel(cols_far, tiles_far, own_far, odd, even, tiles, own, marks, cols, spread, row_sems, sems):
    rows = tiles.shape[0]
    small = [
        pltpu.make_async_copy(cols_far, cols, sems.at[0]),
        pltpu.make_async_copy(own_far, own, sems.at[1]),
    ]
    for copy in small:
        copy.start()
    parts = parts_loaded(rows)

    def part_copy(step):
        some = pl.ds(sum(parts[:step]), parts[step])
        return pltpu.make_async_copy(tiles_far.at[some], tiles.at[some], row_sems.at[step])

    for step in range(len(parts)):
        part_copy(step).start()
    spread[...] = jnp.zeros_like(spread)
    for copy in small:
        copy.wait()
    marks[...] = jnp.full(marks.shape, lax.rem(cols[0, 0] // rows, 2).astype(jnp.float32), jnp.float32)
    for step, number in enumerate(parts):
        part_copy(step).wait()
        spread_rows(cols, tiles, own, spread, sum(parts[:step]), number)
    hand_over(spread, odd, even)


def behind_kernel(cols, tiles, own, odd, even, spread):
    rows = tiles.shape[0]
    spread[...] = jnp.zeros_like(spread)
    together = unrolled(rows)

    def some_rows(step, carry):
        spread_rows(cols, tiles, own, spread, step * together, together)
        return carry

    lax.fori_loop(0, rows // together, some_rows, 0)
    hand_over(spread, odd, even)


def forward_kernel(cols, tiles, own, near, far, other, total, window):
    rows, count, width, _ = tiles.shape
    vectors = own.shape[0]
    window[0] = far[...]
    window[1] = other[1]
    window[2] = near[...]
    window[3] = other[0]
    window[4] = own[...]
    lowest = lowest_row(cols)
    together = unrolled(rows)

    def some_rows(step, carry):
        for start in range(0, together, 2):
            i = step * together + start
            picked = [[], []]
            for j in range(2):
                for k in range(count):
                    column = cols[i + j, k]
                    slot = column - lowest
                    weight = jnp.where(column == cols[i + j, 0], 0.5, 1.0).astype(jnp.bfloat16)
                    block = window[lax.div(slot, rows), :, lanes(lax.rem(slot, rows), width)]
                    picked[j].append(block * weight)
            both = jnp.concatenate([jnp.concatenate(blocks, axis=1) for blocks in picked], axis=0)
            product = lax.dot_general(
                both, stacked_tiles(tiles, i), (((1,), (1,)), ((), ())), preferred_element_type=jnp.float32
            )
            for j in range(2):
                part = product[j * vectors : (j + 1) * vectors, j * width : (j + 1) * width]
                total[:, lanes(i + j, width)] = part
        return carry

    lax.fori_loop(0, rows // together, some_rows, 0)


def cost_of(tiles):
    rows, count, width, _ = tiles.shape
    return pl.CostEstimate(
        flops=2 * rows * count * width * width * 16, bytes_accessed=tiles.size * 2 + MIB, transcendentals=0
    )


SMEM = pl.BlockSpec(memory_space=pltpu.SMEM)
VMEM = pl.BlockSpec(memory_space=pltpu.VMEM)
HBM = pl.BlockSpec(memory_space=pltpu.HBM)


def held(columns, tiles):
    return (
        pltpu.with_memory_space_constraint(columns, pltpu.SMEM),
        pltpu.with_memory_space_constraint(tiles, pltpu.VMEM),
    )


def parts_of(part):
    return jax.ShapeDtypeStruct((2,) + part, jnp.float32), jax.ShapeDtypeStruct((3,) + part, jnp.float32)


def loading(columns, tiles, own):
    part = own.shape
    marks = jax.ShapeDtypeStruct(part, jnp.float32)
    pinned = [pltpu.with_memory_space_constraint(x, pltpu.HBM) for x in (columns, tiles, own)]
    return pl.pallas_call(
        loading_kernel,
        out_shape=parts_of(part) + (pltpu.VMEM(tiles.shape, tiles.dtype), pltpu.VMEM(part, own.dtype), marks, pltpu.SMEM(columns.shape, columns.dtype)),
        in_specs=[HBM] * 3,
        out_specs=(VMEM,) * 5 + (SMEM,),
        scratch_shapes=[
            pltpu.VMEM((SPAN + 1,) + part, jnp.float32),
            pltpu.SemaphoreType.DMA((len(parts_loaded(tiles.shape[0])),)),
            pltpu.SemaphoreType.DMA((2,)),
        ],
        compiler_params=pltpu.CompilerParams(vmem_limit_bytes=24 * MIB),
        cost_estimate=cost_of(tiles),
        name="loading",
    )(*pinned)


def behind(columns, tiles, own):
    part = own.shape
    return pl.pallas_call(
        behind_kernel,
        out_shape=parts_of(part),
        in_specs=[SMEM, VMEM, VMEM],
        out_specs=(VMEM, VMEM),
        scratch_shapes=[pltpu.VMEM((SPAN + 1,) + part, jnp.float32)],
        compiler_params=pltpu.CompilerParams(vmem_limit_bytes=24 * MIB),
        cost_estimate=cost_of(tiles),
        name="behind",
    )(*held(columns, tiles), own)


def forward(columns, tiles, own, near, far, other):
    part = own.shape
    return pl.pallas_call(
        forward_kernel,
        out_shape=jax.ShapeDtypeStruct(part, jnp.float32),
        in_specs=[SMEM] + [VMEM] * 5,
        out_specs=VMEM,
        scratch_shapes=[pltpu.VMEM((SPAN + 1,) + part, own.dtype)],
        compiler_params=pltpu.CompilerParams(vmem_limit_bytes=24 * MIB),
        cost_estimate=cost_of(tiles),
        name="forward",
    )(*held(columns, tiles), own, near, far, other)


def packed(values):
    values = values.astype(jnp.float32)
    largest = jnp.maximum(jnp.max(jnp.abs(values), axis=-1, keepdims=True), 1e-30)
    exponent = jnp.ceil(jnp.log2(largest))
    tail = jnp.broadcast_to(exponent, values.shape[:-1] + (LANES,))
    return jnp.concatenate([values * jnp.exp2(-exponent), tail], axis=-1).astype(jnp.float16)


def unpacked(message):
    width = message.shape[-1] - LANES
    return message[..., :width].astype(jnp.float32) * jnp.exp2(message[..., width : width + 1].astype(jnp.float32))


def per_device(matrix_tiles, columns, vectors, center, halfwidth):
    def fetched(own):
        return rotated(own, 2), rotated(own, 4)

    def applied(own, near, far, odd, even, tiles, second_core, spread_out):
        given = exchanged(odd)
        far, near = lax.optimization_barrier((far, near))
        other = exchanged(jnp.stack([jnp.where(second_core, near, own), jnp.where(second_core, far, near)]))
        kept = even[2] + jnp.where(second_core, 0.0, given[1])
        back = packed(even[:2] + jnp.where(second_core, given, jnp.stack([jnp.zeros_like(kept), given[0]])))
        came_far, came_near = rotated(back[0], -4), rotated(back[1], -2)
        ahead = forward(columns, tiles, own, near, far, other)
        ahead, shift, half = spread_out(ahead)
        ahead, shift, half, came_near, came_far = lax.optimization_barrier((ahead, shift, half, came_near, came_far))
        return ahead + (kept + (unpacked(came_near) + unpacked(came_far))), shift, half

    near, far = fetched(vectors)
    odd, even, tiles, own, marks, columns = loading(columns, matrix_tiles, vectors)
    far, near, odd = lax.optimization_barrier((far, near, odd))
    second_core = marks > 0.5

    def read_scalars(ahead):
        ahead, *scalars = lax.optimization_barrier((ahead, center, halfwidth))
        return (ahead,) + tuple(jnp.broadcast_to(x, ahead.shape) for x in scalars)

    product, centre, half = applied(own, near, far, odd, even, tiles, second_core, read_scalars)
    initial = own.astype(jnp.float32)
    first = (product - centre * initial) / half
    rounded = first.astype(jnp.bfloat16)
    near, far = fetched(rounded)
    odd, even = behind(columns, tiles, rounded)
    product, centre, half = applied(
        rounded, near, far, odd, even, tiles, second_core, lambda ahead: (ahead, centre, half)
    )
    second = 2.0 * (product - centre * first) / half - initial
    return (first, second)


def solution(mesh):
    placed = (P("tri", None, None, None), P("tri", None), P(None, "tri"), P(), P())
    return jax.shard_map(
        per_device,
        mesh=mesh,
        in_specs=placed,
        out_specs=(P(None, "tri"), P(None, "tri")),
        check_vma=False,
    )
```

time: 91.5 us -> 36.1 us (0.39)
  the two profiles are of different devices: /device:TPU:17 before, /device:TPU:0 now
where the time goes in v1:
time: 36.1 us; the launch traced here: 35.9 us
  starting transfers between devices  13.2 us (37%)
  Pallas kernels  9.81 us (27%)
  waiting for transfers between devices  8.72 us (24%)
  between operations  2.12 us (6%)
  other arithmetic  1.89 us (5%)
    ppermute x8, starting transfers between devices, rotated(): lax.ppermute(block, 'tri', [(i, (i + distance) % size) for i in range(siz...  12.5 us
    ppermute x8, waiting for transfers between devices, rotated(): lax.ppermute(block, 'tri', [(i, (i + distance) % size) for i in range(siz...  7.83 us
    pallas_call x1, Pallas kernels, loading(): pl.pallas_call(loading_kernel, out_shape=parts_of(part) + (pltpu.VMEM(til...  4.7 us
    pallas_call x2, Pallas kernels, forward(): pl.pallas_call(forward_kernel, out_shape=jax.ShapeDtypeStruct(part, jnp.f...  3.64 us
    pallas_call x1, Pallas kernels, behind(): pl.pallas_call(behind_kernel, out_shape=parts_of(part), in_specs=[SMEM, V...  1.47 us
    ppermute x4, waiting for transfers between devices, exchanged(): lax.ppermute(block, 'tri', [(i, i ^ 1) for i in range(lax.axis_size('tri'...  0.89 us
    sub x1, other arithmetic, per_device(): second = 2.0 * (product - centre * first) / half - initial  0.78 us
  transfers between devices with their start and end apart: 12, of which 7 were waited for; matrix products, arithmetic and copies ran while one was open for 2% of the time, Pallas kernels for 27%

profile of v1, /device:TPU:0, one launch (start us, length us, event | category | flops | bytes accessed | tf_op | source)
XLA Modules:
  0.0 35.9 jit_solution(3662906753698633625)
XLA Ops:
  0.6 3.0 %collective-permute-start.1 = (bf16[16,2048]{1,0:T(8,128)(2,1)}, bf16[16,2048]{1,0:T(8,128)(2,1)S(1)}, u32[]{:S(2)}, u32[]{:S(2)}) collective-permute-start(bf16[16,2048]{1,0:T(8,128)(2,1)} %own_far.1), channel_id=1, source_target_pairs={{0,2},{1,3},{2,4},{3,5},{4,6},{5,7},{6,8},{7,9},{8,10},{9,11},{10,... | collective-permute-start | bytes 196616 | tf_op jit(solution)/shard_map/ppermute | solution.py:15
  3.6 1.5 %collective-permute-start = (bf16[16,2048]{1,0:T(8,128)(2,1)}, bf16[16,2048]{1,0:T(8,128)(2,1)S(1)}, u32[]{:S(2)}, u32[]{:S(2)}) collective-permute-start(bf16[16,2048]{1,0:T(8,128)(2,1)} %own_far.1), channel_id=1, source_target_pairs={{0,4},{1,5},{2,6},{3,7},{4,8},{5,9},{6,10},{7,11},{8,12},{9,13},{1... | collective-permute-start | bytes 196616 | tf_op jit(solution)/shard_map/ppermute | solution.py:15
  5.1 4.7 %loading.1 = (f32[2,16,2048]{2,1,0:T(8,128)S(1)}, f32[3,16,2048]{2,1,0:T(8,128)S(1)}, bf16[16,12,128,128]{3,2,1,0:T(8,128)(2,1)S(1)}, bf16[16,2048]{1,0:T(8,128)...) custom-call(s32[16,12]{1,0:T(8,128)} %cols_far.1, bf16[16,12,128,128]{3,2,1,0:T(8,128)(2,1)} %tiles_far.1, ...), custom_call_target="tpu_custom_call" | custom-call | flops 100663296 | bytes 7340032 | tf_op jit(solution)/shard_map/loading/pallas_call | solution.py:177
  9.8 1.2 %collective-permute-done.1.near = bf16[16,2048]{1,0:T(8,128)(2,1)S(1)} collective-permute-done((bf16[16,2048]{1,0:T(8,128)(2,1)}, bf16[16,2048]{1,0:T(8,128)(2,1)S(1)}, u32[]{:S(2)}, u32[]{:S(2)}) %collective-permute-start.1) | collective-permute-done | bytes 65568 | tf_op jit(solution)/shard_map/ppermute | solution.py:15
  11.1 0.3 collective-permute-done.far
  11.4 0.6 %collective-permute-start.2 = (bf16[2,16,2048]{2,1,0:T(8,128)(2,1)S(1)}, bf16[2,16,2048]{2,1,0:T(8,128)(2,1)S(1)}, u32[]{:S(2)}, u32[]{:S(2)}) collective-permute-start(bf16[2,16,2048]{2,1,0:T(8,128)(2,1)S(1)} %pad_maximum_fusion), channel_id=1, source_target_pairs={{0,1},{1,0},{2,3},{3,2},{4,5},{5,4},{6,7},{7,6},{8,9},{9,8},{10,11... | collective-permute-start | bytes 393224 | tf_op jit(solution)/shard_map/ppermute | solution.py:19
  12.0 0.9 %collective-permute-done.3 = f32[2,16,2048]{2,1,0:T(8,128)S(1)} collective-permute-done((f32[2,16,2048]{2,1,0:T(8,128)S(1)}, f32[2,16,2048]{2,1,0:T(8,128)S(1)}, u32[]{:S(2)}, u32[]{:S(2)}) %collective-permute-start.3) | collective-permute-done | bytes 262176 | tf_op jit(solution)/shard_map/ppermute | solution.py:19
  12.9 0.1 abs_reduce_fusion.1
  13.0 0.1 multiply_convert_fusion.1
  13.1 0.1 broadcast_in_dim.35
  13.2 1.8 %collective-permute-start.5 = (f16[16,2176]{1,0:T(8,128)(2,1)S(1)}, f16[16,2176]{1,0:T(8,128)(2,1)S(1)}, u32[]{:S(2)}, u32[]{:S(2)}) collective-permute-start(f16[16,2176]{1,0:T(8,128)(2,1)S(1)} %get-tuple-element.64), channel_id=1, source_target_pairs={{0,28},{1,29},{2,30},{3,31},{4,0},{5,1},{6,2},{7,3},{8,4},{9,5},{1... | collective-permute-start | bytes 208904 | tf_op jit(solution)/shard_map/ppermute | solution.py:15
  15.1 1.9 %collective-permute-start.4 = (f16[16,2176]{1,0:T(8,128)(2,1)S(1)}, f16[16,2176]{1,0:T(8,128)(2,1)S(1)}, u32[]{:S(2)}, u32[]{:S(2)}) collective-permute-start(f16[16,2176]{1,0:T(8,128)(2,1)S(1)} %get-tuple-element.65), channel_id=1, source_target_pairs={{0,30},{1,31},{2,0},{3,1},{4,2},{5,3},{6,4},{7,5},{8,6},{9,7},{10,... | collective-permute-start | bytes 208904 | tf_op jit(solution)/shard_map/ppermute | solution.py:15
  18.3 1.8 %forward.2 = f32[16,2048]{1,0:T(8,128)S(1)} custom-call(s32[16,12]{1,0:T(8,128)S(4)} %get-tuple-element.30.cols, bf16[16,12,128,128]{3,2,1,0:T(8,128)(2,1)S(1)} %get-tuple-element.31.tiles, bf16[16,2048]{1,0:T(8,128)(2,1)S(1)} %get-tuple-element.32.own, bf16[16,2048]{1,0:T(8,128)(2,1)S(1)} %collective-permute-done.1.near, ...), custom_call_target="tpu_custom_call" | custom-call | flops 100663296 | bytes 7340032 | tf_op jit(solution)/shard_map/forward/pallas_call | solution.py:209
  20.1 0.1 exponential_reduce_fusion.2
  20.3 0.1 fusion.21
  20.4 1.7 %collective-permute-start.7 = (bf16[16,2048]{1,0:T(8,128)(2,1)S(1)}, bf16[16,2048]{1,0:T(8,128)(2,1)S(1)}, u32[]{:S(2)}, u32[]{:S(2)}) collective-permute-start(bf16[16,2048]{1,0:T(8,128)(2,1)S(1)} %get-tuple-element.58.own), channel_id=1, source_target_pairs={{0,2},{1,3},{2,4},{3,5},{4,6},{5,7},{6,8},{7,9},{8,10},{9,11},{10,... | collective-permute-start | bytes 196616 | tf_op jit(solution)/shard_map/ppermute | solution.py:15
  22.1 0.6 %collective-permute-start.6 = (bf16[16,2048]{1,0:T(8,128)(2,1)S(1)}, bf16[16,2048]{1,0:T(8,128)(2,1)S(1)}, u32[]{:S(2)}, u32[]{:S(2)}) collective-permute-start(bf16[16,2048]{1,0:T(8,128)(2,1)S(1)} %get-tuple-element.58.own), channel_id=1, source_target_pairs={{0,4},{1,5},{2,6},{3,7},{4,8},{5,9},{6,10},{7,11},{8,12},{9,13},{1... | collective-permute-start | bytes 196616 | tf_op jit(solution)/shard_map/ppermute | solution.py:15
  22.7 1.5 %behind.1 = (f32[2,16,2048]{2,1,0:T(8,128)S(1)}, f32[3,16,2048]{2,1,0:T(8,128)S(1)}) custom-call(s32[16,12]{1,0:T(8,128)S(4)} %get-tuple-element.30.cols, bf16[16,12,128,128]{3,2,1,0:T(8,128)(2,1)S(1)} %get-tuple-element.31.tiles, bf16[16,2048]{1,0:T(8,128)(2,1)S(1)} %get-tuple-element.58.own), custom_call_target="tpu_custom_call" | custom-call | flops 100663296 | bytes 7340032 | tf_op jit(solution)/shard_map/behind/pallas_call | solution.py:195
  24.2 0.1 collective-permute-start.9
  24.3 4.2 %collective-permute-done.7.near = bf16[16,2048]{1,0:T(8,128)(2,1)S(1)} collective-permute-done((bf16[16,2048]{1,0:T(8,128)(2,1)S(1)}, bf16[16,2048]{1,0:T(8,128)(2,1)S(1)}, u32[]{:S(2)}, u32[]{:S(2)}) %collective-permute-start.7) | collective-permute-done | bytes 65568 | tf_op jit(solution)/shard_map/ppermute | solution.py:15
  28.5 0.7 %collective-permute-done.6.far = bf16[16,2048]{1,0:T(8,128)(2,1)S(1)} collective-permute-done((bf16[16,2048]{1,0:T(8,128)(2,1)S(1)}, bf16[16,2048]{1,0:T(8,128)(2,1)S(1)}, u32[]{:S(2)}, u32[]{:S(2)}) %collective-permute-start.6) | collective-permute-done | bytes 65568 | tf_op jit(solution)/shard_map/ppermute | solution.py:15
  29.3 0.1 abs_reduce_fusion
  29.4 0.1 multiply_convert_fusion
  29.5 0.1 broadcast_in_dim.37
  29.6 0.9 %collective-permute-start.11 = (f16[16,2176]{1,0:T(8,128)(2,1)S(1)}, f16[16,2176]{1,0:T(8,128)(2,1)S(1)}, u32[]{:S(2)}, u32[]{:S(2)}) collective-permute-start(f16[16,2176]{1,0:T(8,128)(2,1)S(1)} %get-tuple-element.62), channel_id=1, source_target_pairs={{0,28},{1,29},{2,30},{3,31},{4,0},{5,1},{6,2},{7,3},{8,4},{9,5},{1... | collective-permute-start | bytes 208904 | tf_op jit(solution)/shard_map/ppermute | solution.py:15
  30.6 1.0 %collective-permute-start.10 = (f16[16,2176]{1,0:T(8,128)(2,1)S(1)}, f16[16,2176]{1,0:T(8,128)(2,1)S(1)}, u32[]{:S(2)}, u32[]{:S(2)}) collective-permute-start(f16[16,2176]{1,0:T(8,128)(2,1)S(1)} %get-tuple-element.63), channel_id=1, source_target_pairs={{0,30},{1,31},{2,0},{3,1},{4,2},{5,3},{6,4},{7,5},{8,6},{9,7},{10,... | collective-permute-start | bytes 208904 | tf_op jit(solution)/shard_map/ppermute | solution.py:15
  31.6 1.8 %forward.3 = f32[16,2048]{1,0:T(8,128)S(1)} custom-call(s32[16,12]{1,0:T(8,128)S(4)} %get-tuple-element.30.cols, bf16[16,12,128,128]{3,2,1,0:T(8,128)(2,1)S(1)} %get-tuple-element.31.tiles, bf16[16,2048]{1,0:T(8,128)(2,1)S(1)} %get-tuple-element.58.own, bf16[16,2048]{1,0:T(8,128)(2,1)S(1)} %collective-permute-done.7.near, ...), custom_call_target="tpu_custom_call" | custom-call | flops 100663296 | bytes 7340032 | tf_op jit(solution)/shard_map/forward/pallas_call | solution.py:209
  33.4 0.9 %collective-permute-done.11 = f16[16,2176]{1,0:T(8,128)(2,1)S(1)} collective-permute-done((f16[16,2176]{1,0:T(8,128)(2,1)S(1)}, f16[16,2176]{1,0:T(8,128)(2,1)S(1)}, u32[]{:S(2)}, u32[]{:S(2)}) %collective-permute-start.11) | collective-permute-done | bytes 69664 | tf_op jit(solution)/shard_map/ppermute | solution.py:15
  34.3 0.6 %collective-permute-done.10 = f16[16,2176]{1,0:T(8,128)(2,1)S(1)} collective-permute-done((f16[16,2176]{1,0:T(8,128)(2,1)S(1)}, f16[16,2176]{1,0:T(8,128)(2,1)S(1)}, u32[]{:S(2)}, u32[]{:S(2)}) %collective-permute-start.10) | collective-permute-done | bytes 69664 | tf_op jit(solution)/shard_map/ppermute | solution.py:15
  34.9 0.1 exponential_reduce_fusion.1
  35.0 0.1 exponential_reduce_fusion
  35.2 0.8 %convert_subtract_fusion = f32[16,2048]{1,0:T(8,128)} fusion(bf16[16,2048]{1,0:T(8,128)(2,1)S(1)} %get-tuple-element.32.own, f32[16,2048]{1,0:T(8,128)S(1)} %broadcast_in_dim.33, f32[16,2048]{1,0:T(8,128)S(1)} %forward.3, pred[16,2048]{1,0:T(8,128)(4,1)S(1)} %get-tuple-element.61, f32[2,16,2048]{2,1,0:T(8,128)S(1)} %collective-permute-done.9, ...), kind=kLoop, calls=%fused_computation.6 | loop fusion | flops 491520 | bytes 1147008 | tf_op jit(solution)/shard_map/sub | solution.py:268
  (22 shorter events, 0.3 us)
Async XLA Ops:
  0.6 10.4 %collective-permute-start.1 = (bf16[16,2048]{1,0:T(8,128)(2,1)}, bf16[16,2048]{1,0:T(8,128)(2,1)S(1)}, u32[]{:S(2)}, u32[]{:S(2)}) collective-permute-start(bf16[16,2048]{1,0:T(8,128)(2,1)} %own_far.1), channel_id=1, source_target_pairs={{0,2},{1,3},{2,4},{3,5},{4,6},{5,7},{6,8},{7,9},{8,10},{9,11},{10,... | collective-permute-start | bytes 196616 | tf_op jit(solution)/shard_map/ppermute | solution.py:15
  3.6 7.7 %collective-permute-start = (bf16[16,2048]{1,0:T(8,128)(2,1)}, bf16[16,2048]{1,0:T(8,128)(2,1)S(1)}, u32[]{:S(2)}, u32[]{:S(2)}) collective-permute-start(bf16[16,2048]{1,0:T(8,128)(2,1)} %own_far.1), channel_id=1, source_target_pairs={{0,4},{1,5},{2,6},{3,7},{4,8},{5,9},{6,10},{7,11},{8,12},{9,13},{1... | collective-permute-start | bytes 196616 | tf_op jit(solution)/shard_map/ppermute | solution.py:15
  11.3 1.5 %collective-permute-start.3 = (f32[2,16,2048]{2,1,0:T(8,128)S(1)}, f32[2,16,2048]{2,1,0:T(8,128)S(1)}, u32[]{:S(2)}, u32[]{:S(2)}) collective-permute-start(f32[2,16,2048]{2,1,0:T(8,128)S(1)} %get-tuple-element.43), channel_id=1, source_target_pairs={{0,1},{1,0},{2,3},{3,2},{4,5},{5,4},{6,7},{7,6},{8,9},{9,8},{10,11... | collective-permute-start | bytes 786440 | tf_op jit(solution)/shard_map/ppermute | solution.py:19
  11.4 6.9 %collective-permute-start.2 = (bf16[2,16,2048]{2,1,0:T(8,128)(2,1)S(1)}, bf16[2,16,2048]{2,1,0:T(8,128)(2,1)S(1)}, u32[]{:S(2)}, u32[]{:S(2)}) collective-permute-start(bf16[2,16,2048]{2,1,0:T(8,128)(2,1)S(1)} %pad_maximum_fusion), channel_id=1, source_target_pairs={{0,1},{1,0},{2,3},{3,2},{4,5},{5,4},{6,7},{7,6},{8,9},{9,8},{10,11... | collective-permute-start | bytes 393224 | tf_op jit(solution)/shard_map/ppermute | solution.py:19
  13.2 6.9 %collective-permute-start.5 = (f16[16,2176]{1,0:T(8,128)(2,1)S(1)}, f16[16,2176]{1,0:T(8,128)(2,1)S(1)}, u32[]{:S(2)}, u32[]{:S(2)}) collective-permute-start(f16[16,2176]{1,0:T(8,128)(2,1)S(1)} %get-tuple-element.64), channel_id=1, source_target_pairs={{0,28},{1,29},{2,30},{3,31},{4,0},{5,1},{6,2},{7,3},{8,4},{9,5},{1... | collective-permute-start | bytes 208904 | tf_op jit(solution)/shard_map/ppermute | solution.py:15
  15.1 5.0 %collective-permute-start.4 = (f16[16,2176]{1,0:T(8,128)(2,1)S(1)}, f16[16,2176]{1,0:T(8,128)(2,1)S(1)}, u32[]{:S(2)}, u32[]{:S(2)}) collective-permute-start(f16[16,2176]{1,0:T(8,128)(2,1)S(1)} %get-tuple-element.65), channel_id=1, source_target_pairs={{0,30},{1,31},{2,0},{3,1},{4,2},{5,3},{6,4},{7,5},{8,6},{9,7},{10,... | collective-permute-start | bytes 208904 | tf_op jit(solution)/shard_map/ppermute | solution.py:15
  20.4 14.8 %copy-start = (f32[16,2048]{1,0:T(8,128)}, f32[16,2048]{1,0:T(8,128)S(1)}, u32[]{:S(2)}) copy-start(f32[16,2048]{1,0:T(8,128)S(1)} %get-tuple-element.59) | copy-start | bytes 393220
  20.4 8.1 %collective-permute-start.7 = (bf16[16,2048]{1,0:T(8,128)(2,1)S(1)}, bf16[16,2048]{1,0:T(8,128)(2,1)S(1)}, u32[]{:S(2)}, u32[]{:S(2)}) collective-permute-start(bf16[16,2048]{1,0:T(8,128)(2,1)S(1)} %get-tuple-element.58.own), channel_id=1, source_target_pairs={{0,2},{1,3},{2,4},{3,5},{4,6},{5,7},{6,8},{7,9},{8,10},{9,11},{10,... | collective-permute-start | bytes 196616 | tf_op jit(solution)/shard_map/ppermute | solution.py:15
  22.1 7.0 %collective-permute-start.6 = (bf16[16,2048]{1,0:T(8,128)(2,1)S(1)}, bf16[16,2048]{1,0:T(8,128)(2,1)S(1)}, u32[]{:S(2)}, u32[]{:S(2)}) collective-permute-start(bf16[16,2048]{1,0:T(8,128)(2,1)S(1)} %get-tuple-element.58.own), channel_id=1, source_target_pairs={{0,4},{1,5},{2,6},{3,7},{4,8},{5,9},{6,10},{7,11},{8,12},{9,13},{1... | collective-permute-start | bytes 196616 | tf_op jit(solution)/shard_map/ppermute | solution.py:15
  24.2 5.1 %collective-permute-start.9 = (f32[2,16,2048]{2,1,0:T(8,128)S(1)}, f32[2,16,2048]{2,1,0:T(8,128)S(1)}, u32[]{:S(2)}, u32[]{:S(2)}) collective-permute-start(f32[2,16,2048]{2,1,0:T(8,128)S(1)} %get-tuple-element.52), channel_id=1, source_target_pairs={{0,1},{1,0},{2,3},{3,2},{4,5},{5,4},{6,7},{7,6},{8,9},{9,8},{10,11... | collective-permute-start | bytes 786440 | tf_op jit(solution)/shard_map/ppermute | solution.py:19
  29.2 2.4 %collective-permute-start.8 = (bf16[2,16,2048]{2,1,0:T(8,128)(2,1)S(1)}, bf16[2,16,2048]{2,1,0:T(8,128)(2,1)S(1)}, u32[]{:S(2)}, u32[]{:S(2)}) collective-permute-start(bf16[2,16,2048]{2,1,0:T(8,128)(2,1)S(1)} %pad_maximum_fusion.1), channel_id=1, source_target_pairs={{0,1},{1,0},{2,3},{3,2},{4,5},{5,4},{6,7},{7,6},{8,9},{9,8},{10,11... | collective-permute-start | bytes 393224 | tf_op jit(solution)/shard_map/ppermute | solution.py:19
  29.6 4.6 %collective-permute-start.11 = (f16[16,2176]{1,0:T(8,128)(2,1)S(1)}, f16[16,2176]{1,0:T(8,128)(2,1)S(1)}, u32[]{:S(2)}, u32[]{:S(2)}) collective-permute-start(f16[16,2176]{1,0:T(8,128)(2,1)S(1)} %get-tuple-element.62), channel_id=1, source_target_pairs={{0,28},{1,29},{2,30},{3,31},{4,0},{5,1},{6,2},{7,3},{8,4},{9,5},{1... | collective-permute-start | bytes 208904 | tf_op jit(solution)/shard_map/ppermute | solution.py:15
  30.6 4.3 %collective-permute-start.10 = (f16[16,2176]{1,0:T(8,128)(2,1)S(1)}, f16[16,2176]{1,0:T(8,128)(2,1)S(1)}, u32[]{:S(2)}, u32[]{:S(2)}) collective-permute-start(f16[16,2176]{1,0:T(8,128)(2,1)S(1)} %get-tuple-element.63), channel_id=1, source_target_pairs={{0,30},{1,31},{2,0},{3,1},{4,2},{5,3},{6,4},{7,5},{8,6},{9,7},{10,... | collective-permute-start | bytes 208904 | tf_op jit(solution)/shard_map/ppermute | solution.py:15

commit v2 on v1

--- a/solution.py
+++ b/solution.py
@@ -95,8 +95,11 @@
         copy.wait()
     marks[...] = jnp.full(marks.shape, lax.rem(cols[0, 0] // rows, 2).astype(jnp.float32), jnp.float32)
     for step, number in enumerate(parts):
-        part_copy(step).wait()
-        spread_rows(cols, tiles, own, spread, sum(parts[:step]), number)
+        @pl.when(cols[0, 0] >= 0)
+        def _():
+            part_copy(step).wait()
+            spread_rows(cols, tiles, own, spread, sum(parts[:step]), number)
+
     hand_over(spread, odd, even)
 
 

time: 36.1 us -> 36.1 us (level)
  no operation moved by 1% of the time
where the time goes in v2:
time: 36.1 us; the launch traced here: 35.9 us
  starting transfers between devices  13.2 us (37%)
  Pallas kernels  9.82 us (27%)
  waiting for transfers between devices  8.73 us (24%)
  between operations  2.11 us (6%)
  other arithmetic  1.89 us (5%)
    ppermute x8, starting transfers between devices, rotated(): lax.ppermute(block, 'tri', [(i, (i + distance) % size) for i in range(siz...  12.5 us
    ppermute x8, waiting for transfers between devices, rotated(): lax.ppermute(block, 'tri', [(i, (i + distance) % size) for i in range(siz...  7.84 us
    pallas_call x1, Pallas kernels, loading(): pl.pallas_call(loading_kernel, out_shape=parts_of(part) + (pltpu.VMEM(til...  4.71 us
    pallas_call x2, Pallas kernels, forward(): pl.pallas_call(forward_kernel, out_shape=jax.ShapeDtypeStruct(part, jnp.f...  3.64 us
    pallas_call x1, Pallas kernels, behind(): pl.pallas_call(behind_kernel, out_shape=parts_of(part), in_specs=[SMEM, V...  1.47 us
    ppermute x4, waiting for transfers between devices, exchanged(): lax.ppermute(block, 'tri', [(i, i ^ 1) for i in range(lax.axis_size('tri'...  0.89 us
    sub x1, other arithmetic, per_device(): second = 2.0 * (product - centre * first) / half - initial  0.78 us
  transfers between devices with their start and end apart: 12, of which 7 were waited for; matrix products, arithmetic and copies ran while one was open for 2% of the time, Pallas kernels for 27%

profile of v2, /device:TPU:0, one launch (start us, length us, event | category | flops | bytes accessed | tf_op | source)
XLA Modules:
  0.0 35.9 jit_solution(4072171299831616195)
XLA Ops:
  0.6 3.0 %collective-permute-start.1 = (bf16[16,2048]{1,0:T(8,128)(2,1)}, bf16[16,2048]{1,0:T(8,128)(2,1)S(1)}, u32[]{:S(2)}, u32[]{:S(2)}) collective-permute-start(bf16[16,2048]{1,0:T(8,128)(2,1)} %own_far.1), channel_id=1, source_target_pairs={{0,2},{1,3},{2,4},{3,5},{4,6},{5,7},{6,8},{7,9},{8,10},{9,11},{10,... | collective-permute-start | bytes 196616 | tf_op jit(solution)/shard_map/ppermute | solution.py:15
  3.6 1.5 %collective-permute-start = (bf16[16,2048]{1,0:T(8,128)(2,1)}, bf16[16,2048]{1,0:T(8,128)(2,1)S(1)}, u32[]{:S(2)}, u32[]{:S(2)}) collective-permute-start(bf16[16,2048]{1,0:T(8,128)(2,1)} %own_far.1), channel_id=1, source_target_pairs={{0,4},{1,5},{2,6},{3,7},{4,8},{5,9},{6,10},{7,11},{8,12},{9,13},{1... | collective-permute-start | bytes 196616 | tf_op jit(solution)/shard_map/ppermute | solution.py:15
  5.1 4.7 %loading.1 = (f32[2,16,2048]{2,1,0:T(8,128)S(1)}, f32[3,16,2048]{2,1,0:T(8,128)S(1)}, bf16[16,12,128,128]{3,2,1,0:T(8,128)(2,1)S(1)}, bf16[16,2048]{1,0:T(8,128)...) custom-call(s32[16,12]{1,0:T(8,128)} %cols_far.1, bf16[16,12,128,128]{3,2,1,0:T(8,128)(2,1)} %tiles_far.1, ...), custom_call_target="tpu_custom_call" | custom-call | flops 100663296 | bytes 7340032 | tf_op jit(solution)/shard_map/loading/pallas_call | solution.py:180
  9.9 1.2 %collective-permute-done.1.near = bf16[16,2048]{1,0:T(8,128)(2,1)S(1)} collective-permute-done((bf16[16,2048]{1,0:T(8,128)(2,1)}, bf16[16,2048]{1,0:T(8,128)(2,1)S(1)}, u32[]{:S(2)}, u32[]{:S(2)}) %collective-permute-start.1) | collective-permute-done | bytes 65568 | tf_op jit(solution)/shard_map/ppermute | solution.py:15
  11.1 0.3 collective-permute-done.far
  11.4 0.6 %collective-permute-start.2 = (bf16[2,16,2048]{2,1,0:T(8,128)(2,1)S(1)}, bf16[2,16,2048]{2,1,0:T(8,128)(2,1)S(1)}, u32[]{:S(2)}, u32[]{:S(2)}) collective-permute-start(bf16[2,16,2048]{2,1,0:T(8,128)(2,1)S(1)} %pad_maximum_fusion), channel_id=1, source_target_pairs={{0,1},{1,0},{2,3},{3,2},{4,5},{5,4},{6,7},{7,6},{8,9},{9,8},{10,11... | collective-permute-start | bytes 393224 | tf_op jit(solution)/shard_map/ppermute | solution.py:19
  12.0 0.9 %collective-permute-done.3 = f32[2,16,2048]{2,1,0:T(8,128)S(1)} collective-permute-done((f32[2,16,2048]{2,1,0:T(8,128)S(1)}, f32[2,16,2048]{2,1,0:T(8,128)S(1)}, u32[]{:S(2)}, u32[]{:S(2)}) %collective-permute-start.3) | collective-permute-done | bytes 262176 | tf_op jit(solution)/shard_map/ppermute | solution.py:19
  12.9 0.1 abs_reduce_fusion.1
  13.0 0.1 multiply_convert_fusion.1
  13.1 0.1 broadcast_in_dim.35
  13.2 1.9 %collective-permute-start.5 = (f16[16,2176]{1,0:T(8,128)(2,1)S(1)}, f16[16,2176]{1,0:T(8,128)(2,1)S(1)}, u32[]{:S(2)}, u32[]{:S(2)}) collective-permute-start(f16[16,2176]{1,0:T(8,128)(2,1)S(1)} %get-tuple-element.64), channel_id=1, source_target_pairs={{0,28},{1,29},{2,30},{3,31},{4,0},{5,1},{6,2},{7,3},{8,4},{9,5},{1... | collective-permute-start | bytes 208904 | tf_op jit(solution)/shard_map/ppermute | solution.py:15
  15.1 1.9 %collective-permute-start.4 = (f16[16,2176]{1,0:T(8,128)(2,1)S(1)}, f16[16,2176]{1,0:T(8,128)(2,1)S(1)}, u32[]{:S(2)}, u32[]{:S(2)}) collective-permute-start(f16[16,2176]{1,0:T(8,128)(2,1)S(1)} %get-tuple-element.65), channel_id=1, source_target_pairs={{0,30},{1,31},{2,0},{3,1},{4,2},{5,3},{6,4},{7,5},{8,6},{9,7},{10,... | collective-permute-start | bytes 208904 | tf_op jit(solution)/shard_map/ppermute | solution.py:15
  18.3 1.8 %forward.2 = f32[16,2048]{1,0:T(8,128)S(1)} custom-call(s32[16,12]{1,0:T(8,128)S(4)} %get-tuple-element.30.cols, bf16[16,12,128,128]{3,2,1,0:T(8,128)(2,1)S(1)} %get-tuple-element.31.tiles, bf16[16,2048]{1,0:T(8,128)(2,1)S(1)} %get-tuple-element.32.own, bf16[16,2048]{1,0:T(8,128)(2,1)S(1)} %collective-permute-done.1.near, ...), custom_call_target="tpu_custom_call" | custom-call | flops 100663296 | bytes 7340032 | tf_op jit(solution)/shard_map/forward/pallas_call | solution.py:212
  20.1 0.1 exponential_reduce_fusion.2
  20.3 0.1 fusion.21
  20.4 1.7 %collective-permute-start.7 = (bf16[16,2048]{1,0:T(8,128)(2,1)S(1)}, bf16[16,2048]{1,0:T(8,128)(2,1)S(1)}, u32[]{:S(2)}, u32[]{:S(2)}) collective-permute-start(bf16[16,2048]{1,0:T(8,128)(2,1)S(1)} %get-tuple-element.58.own), channel_id=1, source_target_pairs={{0,2},{1,3},{2,4},{3,5},{4,6},{5,7},{6,8},{7,9},{8,10},{9,11},{10,... | collective-permute-start | bytes 196616 | tf_op jit(solution)/shard_map/ppermute | solution.py:15
  22.1 0.6 %collective-permute-start.6 = (bf16[16,2048]{1,0:T(8,128)(2,1)S(1)}, bf16[16,2048]{1,0:T(8,128)(2,1)S(1)}, u32[]{:S(2)}, u32[]{:S(2)}) collective-permute-start(bf16[16,2048]{1,0:T(8,128)(2,1)S(1)} %get-tuple-element.58.own), channel_id=1, source_target_pairs={{0,4},{1,5},{2,6},{3,7},{4,8},{5,9},{6,10},{7,11},{8,12},{9,13},{1... | collective-permute-start | bytes 196616 | tf_op jit(solution)/shard_map/ppermute | solution.py:15
  22.7 1.5 %behind.1 = (f32[2,16,2048]{2,1,0:T(8,128)S(1)}, f32[3,16,2048]{2,1,0:T(8,128)S(1)}) custom-call(s32[16,12]{1,0:T(8,128)S(4)} %get-tuple-element.30.cols, bf16[16,12,128,128]{3,2,1,0:T(8,128)(2,1)S(1)} %get-tuple-element.31.tiles, bf16[16,2048]{1,0:T(8,128)(2,1)S(1)} %get-tuple-element.58.own), custom_call_target="tpu_custom_call" | custom-call | flops 100663296 | bytes 7340032 | tf_op jit(solution)/shard_map/behind/pallas_call | solution.py:198
  24.2 0.1 collective-permute-start.9
  24.3 4.2 %collective-permute-done.7.near = bf16[16,2048]{1,0:T(8,128)(2,1)S(1)} collective-permute-done((bf16[16,2048]{1,0:T(8,128)(2,1)S(1)}, bf16[16,2048]{1,0:T(8,128)(2,1)S(1)}, u32[]{:S(2)}, u32[]{:S(2)}) %collective-permute-start.7) | collective-permute-done | bytes 65568 | tf_op jit(solution)/shard_map/ppermute | solution.py:15
  28.5 0.7 %collective-permute-done.6.far = bf16[16,2048]{1,0:T(8,128)(2,1)S(1)} collective-permute-done((bf16[16,2048]{1,0:T(8,128)(2,1)S(1)}, bf16[16,2048]{1,0:T(8,128)(2,1)S(1)}, u32[]{:S(2)}, u32[]{:S(2)}) %collective-permute-start.6) | collective-permute-done | bytes 65568 | tf_op jit(solution)/shard_map/ppermute | solution.py:15
  29.3 0.1 abs_reduce_fusion
  29.4 0.1 multiply_convert_fusion
  29.6 0.1 broadcast_in_dim.37
  29.7 0.9 %collective-permute-start.11 = (f16[16,2176]{1,0:T(8,128)(2,1)S(1)}, f16[16,2176]{1,0:T(8,128)(2,1)S(1)}, u32[]{:S(2)}, u32[]{:S(2)}) collective-permute-start(f16[16,2176]{1,0:T(8,128)(2,1)S(1)} %get-tuple-element.62), channel_id=1, source_target_pairs={{0,28},{1,29},{2,30},{3,31},{4,0},{5,1},{6,2},{7,3},{8,4},{9,5},{1... | collective-permute-start | bytes 208904 | tf_op jit(solution)/shard_map/ppermute | solution.py:15
  30.6 1.0 %collective-permute-start.10 = (f16[16,2176]{1,0:T(8,128)(2,1)S(1)}, f16[16,2176]{1,0:T(8,128)(2,1)S(1)}, u32[]{:S(2)}, u32[]{:S(2)}) collective-permute-start(f16[16,2176]{1,0:T(8,128)(2,1)S(1)} %get-tuple-element.63), channel_id=1, source_target_pairs={{0,30},{1,31},{2,0},{3,1},{4,2},{5,3},{6,4},{7,5},{8,6},{9,7},{10,... | collective-permute-start | bytes 208904 | tf_op jit(solution)/shard_map/ppermute | solution.py:15
  31.6 1.8 %forward.3 = f32[16,2048]{1,0:T(8,128)S(1)} custom-call(s32[16,12]{1,0:T(8,128)S(4)} %get-tuple-element.30.cols, bf16[16,12,128,128]{3,2,1,0:T(8,128)(2,1)S(1)} %get-tuple-element.31.tiles, bf16[16,2048]{1,0:T(8,128)(2,1)S(1)} %get-tuple-element.58.own, bf16[16,2048]{1,0:T(8,128)(2,1)S(1)} %collective-permute-done.7.near, ...), custom_call_target="tpu_custom_call" | custom-call | flops 100663296 | bytes 7340032 | tf_op jit(solution)/shard_map/forward/pallas_call | solution.py:212
  33.4 0.9 %collective-permute-done.11 = f16[16,2176]{1,0:T(8,128)(2,1)S(1)} collective-permute-done((f16[16,2176]{1,0:T(8,128)(2,1)S(1)}, f16[16,2176]{1,0:T(8,128)(2,1)S(1)}, u32[]{:S(2)}, u32[]{:S(2)}) %collective-permute-start.11) | collective-permute-done | bytes 69664 | tf_op jit(solution)/shard_map/ppermute | solution.py:15
  34.3 0.6 %collective-permute-done.10 = f16[16,2176]{1,0:T(8,128)(2,1)S(1)} collective-permute-done((f16[16,2176]{1,0:T(8,128)(2,1)S(1)}, f16[16,2176]{1,0:T(8,128)(2,1)S(1)}, u32[]{:S(2)}, u32[]{:S(2)}) %collective-permute-start.10) | collective-permute-done | bytes 69664 | tf_op jit(solution)/shard_map/ppermute | solution.py:15
  34.9 0.1 exponential_reduce_fusion.1
  35.0 0.1 exponential_reduce_fusion
  35.2 0.8 %convert_subtract_fusion = f32[16,2048]{1,0:T(8,128)} fusion(bf16[16,2048]{1,0:T(8,128)(2,1)S(1)} %get-tuple-element.32.own, f32[16,2048]{1,0:T(8,128)S(1)} %broadcast_in_dim.33, f32[16,2048]{1,0:T(8,128)S(1)} %forward.3, pred[16,2048]{1,0:T(8,128)(4,1)S(1)} %get-tuple-element.61, f32[2,16,2048]{2,1,0:T(8,128)S(1)} %collective-permute-done.9, ...), kind=kLoop, calls=%fused_computation.6 | loop fusion | flops 491520 | bytes 1147008 | tf_op jit(solution)/shard_map/sub | solution.py:271
  (22 shorter events, 0.3 us)
Async XLA Ops:
  0.6 10.4 %collective-permute-start.1 = (bf16[16,2048]{1,0:T(8,128)(2,1)}, bf16[16,2048]{1,0:T(8,128)(2,1)S(1)}, u32[]{:S(2)}, u32[]{:S(2)}) collective-permute-start(bf16[16,2048]{1,0:T(8,128)(2,1)} %own_far.1), channel_id=1, source_target_pairs={{0,2},{1,3},{2,4},{3,5},{4,6},{5,7},{6,8},{7,9},{8,10},{9,11},{10,... | collective-permute-start | bytes 196616 | tf_op jit(solution)/shard_map/ppermute | solution.py:15
  3.6 7.7 %collective-permute-start = (bf16[16,2048]{1,0:T(8,128)(2,1)}, bf16[16,2048]{1,0:T(8,128)(2,1)S(1)}, u32[]{:S(2)}, u32[]{:S(2)}) collective-permute-start(bf16[16,2048]{1,0:T(8,128)(2,1)} %own_far.1), channel_id=1, source_target_pairs={{0,4},{1,5},{2,6},{3,7},{4,8},{5,9},{6,10},{7,11},{8,12},{9,13},{1... | collective-permute-start | bytes 196616 | tf_op jit(solution)/shard_map/ppermute | solution.py:15
  11.3 1.5 %collective-permute-start.3 = (f32[2,16,2048]{2,1,0:T(8,128)S(1)}, f32[2,16,2048]{2,1,0:T(8,128)S(1)}, u32[]{:S(2)}, u32[]{:S(2)}) collective-permute-start(f32[2,16,2048]{2,1,0:T(8,128)S(1)} %get-tuple-element.43), channel_id=1, source_target_pairs={{0,1},{1,0},{2,3},{3,2},{4,5},{5,4},{6,7},{7,6},{8,9},{9,8},{10,11... | collective-permute-start | bytes 786440 | tf_op jit(solution)/shard_map/ppermute | solution.py:19
  11.4 6.9 %collective-permute-start.2 = (bf16[2,16,2048]{2,1,0:T(8,128)(2,1)S(1)}, bf16[2,16,2048]{2,1,0:T(8,128)(2,1)S(1)}, u32[]{:S(2)}, u32[]{:S(2)}) collective-permute-start(bf16[2,16,2048]{2,1,0:T(8,128)(2,1)S(1)} %pad_maximum_fusion), channel_id=1, source_target_pairs={{0,1},{1,0},{2,3},{3,2},{4,5},{5,4},{6,7},{7,6},{8,9},{9,8},{10,11... | collective-permute-start | bytes 393224 | tf_op jit(solution)/shard_map/ppermute | solution.py:19
  13.2 6.9 %collective-permute-start.5 = (f16[16,2176]{1,0:T(8,128)(2,1)S(1)}, f16[16,2176]{1,0:T(8,128)(2,1)S(1)}, u32[]{:S(2)}, u32[]{:S(2)}) collective-permute-start(f16[16,2176]{1,0:T(8,128)(2,1)S(1)} %get-tuple-element.64), channel_id=1, source_target_pairs={{0,28},{1,29},{2,30},{3,31},{4,0},{5,1},{6,2},{7,3},{8,4},{9,5},{1... | collective-permute-start | bytes 208904 | tf_op jit(solution)/shard_map/ppermute | solution.py:15
  15.1 5.0 %collective-permute-start.4 = (f16[16,2176]{1,0:T(8,128)(2,1)S(1)}, f16[16,2176]{1,0:T(8,128)(2,1)S(1)}, u32[]{:S(2)}, u32[]{:S(2)}) collective-permute-start(f16[16,2176]{1,0:T(8,128)(2,1)S(1)} %get-tuple-element.65), channel_id=1, source_target_pairs={{0,30},{1,31},{2,0},{3,1},{4,2},{5,3},{6,4},{7,5},{8,6},{9,7},{10,... | collective-permute-start | bytes 208904 | tf_op jit(solution)/shard_map/ppermute | solution.py:15
  20.4 14.8 %copy-start = (f32[16,2048]{1,0:T(8,128)}, f32[16,2048]{1,0:T(8,128)S(1)}, u32[]{:S(2)}) copy-start(f32[16,2048]{1,0:T(8,128)S(1)} %get-tuple-element.59) | copy-start | bytes 393220
  20.4 8.1 %collective-permute-start.7 = (bf16[16,2048]{1,0:T(8,128)(2,1)S(1)}, bf16[16,2048]{1,0:T(8,128)(2,1)S(1)}, u32[]{:S(2)}, u32[]{:S(2)}) collective-permute-start(bf16[16,2048]{1,0:T(8,128)(2,1)S(1)} %get-tuple-element.58.own), channel_id=1, source_target_pairs={{0,2},{1,3},{2,4},{3,5},{4,6},{5,7},{6,8},{7,9},{8,10},{9,11},{10,... | collective-permute-start | bytes 196616 | tf_op jit(solution)/shard_map/ppermute | solution.py:15
  22.1 7.0 %collective-permute-start.6 = (bf16[16,2048]{1,0:T(8,128)(2,1)S(1)}, bf16[16,2048]{1,0:T(8,128)(2,1)S(1)}, u32[]{:S(2)}, u32[]{:S(2)}) collective-permute-start(bf16[16,2048]{1,0:T(8,128)(2,1)S(1)} %get-tuple-element.58.own), channel_id=1, source_target_pairs={{0,4},{1,5},{2,6},{3,7},{4,8},{5,9},{6,10},{7,11},{8,12},{9,13},{1... | collective-permute-start | bytes 196616 | tf_op jit(solution)/shard_map/ppermute | solution.py:15
  24.2 5.1 %collective-permute-start.9 = (f32[2,16,2048]{2,1,0:T(8,128)S(1)}, f32[2,16,2048]{2,1,0:T(8,128)S(1)}, u32[]{:S(2)}, u32[]{:S(2)}) collective-permute-start(f32[2,16,2048]{2,1,0:T(8,128)S(1)} %get-tuple-element.52), channel_id=1, source_target_pairs={{0,1},{1,0},{2,3},{3,2},{4,5},{5,4},{6,7},{7,6},{8,9},{9,8},{10,11... | collective-permute-start | bytes 786440 | tf_op jit(solution)/shard_map/ppermute | solution.py:19
  29.2 2.4 %collective-permute-start.8 = (bf16[2,16,2048]{2,1,0:T(8,128)(2,1)S(1)}, bf16[2,16,2048]{2,1,0:T(8,128)(2,1)S(1)}, u32[]{:S(2)}, u32[]{:S(2)}) collective-permute-start(bf16[2,16,2048]{2,1,0:T(8,128)(2,1)S(1)} %pad_maximum_fusion.1), channel_id=1, source_target_pairs={{0,1},{1,0},{2,3},{3,2},{4,5},{5,4},{6,7},{7,6},{8,9},{9,8},{10,11... | collective-permute-start | bytes 393224 | tf_op jit(solution)/shard_map/ppermute | solution.py:19
  29.7 4.6 %collective-permute-start.11 = (f16[16,2176]{1,0:T(8,128)(2,1)S(1)}, f16[16,2176]{1,0:T(8,128)(2,1)S(1)}, u32[]{:S(2)}, u32[]{:S(2)}) collective-permute-start(f16[16,2176]{1,0:T(8,128)(2,1)S(1)} %get-tuple-element.62), channel_id=1, source_target_pairs={{0,28},{1,29},{2,30},{3,31},{4,0},{5,1},{6,2},{7,3},{8,4},{9,5},{1... | collective-permute-start | bytes 208904 | tf_op jit(solution)/shard_map/ppermute | solution.py:15
  30.6 4.3 %collective-permute-start.10 = (f16[16,2176]{1,0:T(8,128)(2,1)S(1)}, f16[16,2176]{1,0:T(8,128)(2,1)S(1)}, u32[]{:S(2)}, u32[]{:S(2)}) collective-permute-start(f16[16,2176]{1,0:T(8,128)(2,1)S(1)} %get-tuple-element.63), channel_id=1, source_target_pairs={{0,30},{1,31},{2,0},{3,1},{4,2},{5,3},{6,4},{7,5},{8,6},{9,7},{10,... | collective-permute-start | bytes 208904 | tf_op jit(solution)/shard_map/ppermute | solution.py:15

commit v3 on v2

--- a/solution.py
+++ b/solution.py
@@ -234,21 +234,29 @@
     return message[..., :width].astype(jnp.float32) * jnp.exp2(message[..., width : width + 1].astype(jnp.float32))
 
 
+def rounded_to_send(values):
+    return values.astype(jnp.bfloat16)
+
+
+def widened(message):
+    return message.astype(jnp.float32)
+
+
 def per_device(matrix_tiles, columns, vectors, center, halfwidth):
     def fetched(own):
         return rotated(own, 2), rotated(own, 4)
 
-    def applied(own, near, far, odd, even, tiles, second_core, spread_out):
+    def applied(own, near, far, odd, even, tiles, second_core, spread_out, pack, unpack):
         given = exchanged(odd)
         far, near = lax.optimization_barrier((far, near))
         other = exchanged(jnp.stack([jnp.where(second_core, near, own), jnp.where(second_core, far, near)]))
         kept = even[2] + jnp.where(second_core, 0.0, given[1])
-        back = packed(even[:2] + jnp.where(second_core, given, jnp.stack([jnp.zeros_like(kept), given[0]])))
+        back = pack(even[:2] + jnp.where(second_core, given, jnp.stack([jnp.zeros_like(kept), given[0]])))
         came_far, came_near = rotated(back[0], -4), rotated(back[1], -2)
         ahead = forward(columns, tiles, own, near, far, other)
         ahead, shift, half = spread_out(ahead)
         ahead, shift, half, came_near, came_far = lax.optimization_barrier((ahead, shift, half, came_near, came_far))
-        return ahead + (kept + (unpacked(came_near) + unpacked(came_far))), shift, half
+        return ahead + (kept + (unpack(came_near) + unpack(came_far))), shift, half
 
     near, far = fetched(vectors)
     odd, even, tiles, own, marks, columns = loading(columns, matrix_tiles, vectors)
@@ -259,14 +267,14 @@
         ahead, *scalars = lax.optimization_barrier((ahead, center, halfwidth))
         return (ahead,) + tuple(jnp.broadcast_to(x, ahead.shape) for x in scalars)
 
-    product, centre, half = applied(own, near, far, odd, even, tiles, second_core, read_scalars)
+    product, centre, half = applied(own, near, far, odd, even, tiles, second_core, read_scalars, packed, unpacked)
     initial = own.astype(jnp.float32)
     first = (product - centre * initial) / half
     rounded = first.astype(jnp.bfloat16)
     near, far = fetched(rounded)
     odd, even = behind(columns, tiles, rounded)
     product, centre, half = applied(
-        rounded, near, far, odd, even, tiles, second_core, lambda ahead: (ahead, centre, half)
+        rounded, near, far, odd, even, tiles, second_core, lambda ahead: (ahead, centre, half), rounded_to_send, widened
     )
     second = 2.0 * (product - centre * first) / half - initial
     return (first, second)

time: 36.1 us -> 35.5 us (0.983)
  other arithmetic: 1.89 us -> 1.37 us
  transfers between devices with their start and end apart: 12 -> 12, of which waited for: 7 -> 7; matrix products, arithmetic and copies ran while one was open for 2% -> 1% of each run, Pallas kernels for 27% -> 28%
where the time goes in v3:
time: 35.5 us; the launch traced here: 35.3 us
  starting transfers between devices  13.2 us (37%)
  Pallas kernels  9.82 us (28%)
  waiting for transfers between devices  8.68 us (24%)
  between operations  2.1 us (6%)
  other arithmetic  1.37 us (4%)
    ppermute x8, starting transfers between devices, rotated(): lax.ppermute(block, 'tri', [(i, (i + distance) % size) for i in range(siz...  12.5 us
    ppermute x8, waiting for transfers between devices, rotated(): lax.ppermute(block, 'tri', [(i, (i + distance) % size) for i in range(siz...  7.79 us
    pallas_call x1, Pallas kernels, loading(): pl.pallas_call(loading_kernel, out_shape=parts_of(part) + (pltpu.VMEM(til...  4.72 us
    pallas_call x2, Pallas kernels, forward(): pl.pallas_call(forward_kernel, out_shape=jax.ShapeDtypeStruct(part, jnp.f...  3.64 us
    pallas_call x1, Pallas kernels, behind(): pl.pallas_call(behind_kernel, out_shape=parts_of(part), in_specs=[SMEM, V...  1.47 us
    ppermute x4, waiting for transfers between devices, exchanged(): lax.ppermute(block, 'tri', [(i, i ^ 1) for i in range(lax.axis_size('tri'...  0.89 us
    sub x1, other arithmetic, per_device(): second = 2.0 * (product - centre * first) / half - initial  0.73 us
    ppermute x4, starting transfers between devices, exchanged(): lax.ppermute(block, 'tri', [(i, i ^ 1) for i in range(lax.axis_size('tri'...  0.72 us
  transfers between devices with their start and end apart: 12, of which 7 were waited for; matrix products, arithmetic and copies ran while one was open for 1% of the time, Pallas kernels for 28%

profile of v3, /device:TPU:0, one launch (start us, length us, event | category | flops | bytes accessed | tf_op | source)
XLA Modules:
  0.0 35.3 jit_solution(11084142279710073796)
XLA Ops:
  0.6 3.0 %collective-permute-start.1 = (bf16[16,2048]{1,0:T(8,128)(2,1)}, bf16[16,2048]{1,0:T(8,128)(2,1)S(1)}, u32[]{:S(2)}, u32[]{:S(2)}) collective-permute-start(bf16[16,2048]{1,0:T(8,128)(2,1)} %own_far.1), channel_id=1, source_target_pairs={{0,2},{1,3},{2,4},{3,5},{4,6},{5,7},{6,8},{7,9},{8,10},{9,11},{10,... | collective-permute-start | bytes 196616 | tf_op jit(solution)/shard_map/ppermute | solution.py:15
  3.6 1.5 %collective-permute-start = (bf16[16,2048]{1,0:T(8,128)(2,1)}, bf16[16,2048]{1,0:T(8,128)(2,1)S(1)}, u32[]{:S(2)}, u32[]{:S(2)}) collective-permute-start(bf16[16,2048]{1,0:T(8,128)(2,1)} %own_far.1), channel_id=1, source_target_pairs={{0,4},{1,5},{2,6},{3,7},{4,8},{5,9},{6,10},{7,11},{8,12},{9,13},{1... | collective-permute-start | bytes 196616 | tf_op jit(solution)/shard_map/ppermute | solution.py:15
  5.1 4.7 %loading.1 = (f32[2,16,2048]{2,1,0:T(8,128)S(1)}, f32[3,16,2048]{2,1,0:T(8,128)S(1)}, bf16[16,12,128,128]{3,2,1,0:T(8,128)(2,1)S(1)}, bf16[16,2048]{1,0:T(8,128)...) custom-call(s32[16,12]{1,0:T(8,128)} %cols_far.1, bf16[16,12,128,128]{3,2,1,0:T(8,128)(2,1)} %tiles_far.1, ...), custom_call_target="tpu_custom_call" | custom-call | flops 100663296 | bytes 7340032 | tf_op jit(solution)/shard_map/loading/pallas_call | solution.py:180
  9.9 1.2 %collective-permute-done.1.near = bf16[16,2048]{1,0:T(8,128)(2,1)S(1)} collective-permute-done((bf16[16,2048]{1,0:T(8,128)(2,1)}, bf16[16,2048]{1,0:T(8,128)(2,1)S(1)}, u32[]{:S(2)}, u32[]{:S(2)}) %collective-permute-start.1) | collective-permute-done | bytes 65568 | tf_op jit(solution)/shard_map/ppermute | solution.py:15
  11.1 0.3 collective-permute-done.far
  11.3 0.0 collective-permute-start.3
  11.4 0.6 %collective-permute-start.2 = (bf16[2,16,2048]{2,1,0:T(8,128)(2,1)S(1)}, bf16[2,16,2048]{2,1,0:T(8,128)(2,1)S(1)}, u32[]{:S(2)}, u32[]{:S(2)}) collective-permute-start(bf16[2,16,2048]{2,1,0:T(8,128)(2,1)S(1)} %pad_maximum_fusion), channel_id=1, source_target_pairs={{0,1},{1,0},{2,3},{3,2},{4,5},{5,4},{6,7},{7,6},{8,9},{9,8},{10,11... | collective-permute-start | bytes 393224 | tf_op jit(solution)/shard_map/ppermute | solution.py:19
  12.0 0.9 %collective-permute-done.3 = f32[2,16,2048]{2,1,0:T(8,128)S(1)} collective-permute-done((f32[2,16,2048]{2,1,0:T(8,128)S(1)}, f32[2,16,2048]{2,1,0:T(8,128)S(1)}, u32[]{:S(2)}, u32[]{:S(2)}) %collective-permute-start.3) | collective-permute-done | bytes 262176 | tf_op jit(solution)/shard_map/ppermute | solution.py:19
  12.9 0.1 abs_reduce_fusion
  13.0 0.1 multiply_convert_fusion
  13.1 0.1 broadcast_in_dim.29
  13.2 1.9 %collective-permute-start.5 = (f16[16,2176]{1,0:T(8,128)(2,1)S(1)}, f16[16,2176]{1,0:T(8,128)(2,1)S(1)}, u32[]{:S(2)}, u32[]{:S(2)}) collective-permute-start(f16[16,2176]{1,0:T(8,128)(2,1)S(1)} %get-tuple-element.62), channel_id=1, source_target_pairs={{0,28},{1,29},{2,30},{3,31},{4,0},{5,1},{6,2},{7,3},{8,4},{9,5},{1... | collective-permute-start | bytes 208904 | tf_op jit(solution)/shard_map/ppermute | solution.py:15
  15.1 1.9 %collective-permute-start.4 = (f16[16,2176]{1,0:T(8,128)(2,1)S(1)}, f16[16,2176]{1,0:T(8,128)(2,1)S(1)}, u32[]{:S(2)}, u32[]{:S(2)}) collective-permute-start(f16[16,2176]{1,0:T(8,128)(2,1)S(1)} %get-tuple-element.63), channel_id=1, source_target_pairs={{0,30},{1,31},{2,0},{3,1},{4,2},{5,3},{6,4},{7,5},{8,6},{9,7},{10,... | collective-permute-start | bytes 208904 | tf_op jit(solution)/shard_map/ppermute | solution.py:15
  18.3 0.0 collective-permute-done.2.other
  18.3 1.8 %forward.2 = f32[16,2048]{1,0:T(8,128)S(1)} custom-call(s32[16,12]{1,0:T(8,128)S(4)} %get-tuple-element.30.cols, bf16[16,12,128,128]{3,2,1,0:T(8,128)(2,1)S(1)} %get-tuple-element.31.tiles, bf16[16,2048]{1,0:T(8,128)(2,1)S(1)} %get-tuple-element.32.own, bf16[16,2048]{1,0:T(8,128)(2,1)S(1)} %collective-permute-done.1.near, ...), custom_call_target="tpu_custom_call" | custom-call | flops 100663296 | bytes 7340032 | tf_op jit(solution)/shard_map/forward/pallas_call | solution.py:212
  20.1 0.0 collective-permute-done.5
  20.1 0.1 exponential_reduce_fusion
  20.3 0.1 fusion.17
  20.4 0.0 copy-start
  20.4 1.7 %collective-permute-start.7 = (bf16[16,2048]{1,0:T(8,128)(2,1)S(1)}, bf16[16,2048]{1,0:T(8,128)(2,1)S(1)}, u32[]{:S(2)}, u32[]{:S(2)}) collective-permute-start(bf16[16,2048]{1,0:T(8,128)(2,1)S(1)} %get-tuple-element.58.own), channel_id=1, source_target_pairs={{0,2},{1,3},{2,4},{3,5},{4,6},{5,7},{6,8},{7,9},{8,10},{9,11},{10,... | collective-permute-start | bytes 196616 | tf_op jit(solution)/shard_map/ppermute | solution.py:15
  22.1 0.6 %collective-permute-start.6 = (bf16[16,2048]{1,0:T(8,128)(2,1)S(1)}, bf16[16,2048]{1,0:T(8,128)(2,1)S(1)}, u32[]{:S(2)}, u32[]{:S(2)}) collective-permute-start(bf16[16,2048]{1,0:T(8,128)(2,1)S(1)} %get-tuple-element.58.own), channel_id=1, source_target_pairs={{0,4},{1,5},{2,6},{3,7},{4,8},{5,9},{6,10},{7,11},{8,12},{9,13},{1... | collective-permute-start | bytes 196616 | tf_op jit(solution)/shard_map/ppermute | solution.py:15
  22.7 1.5 %behind.1 = (f32[2,16,2048]{2,1,0:T(8,128)S(1)}, f32[3,16,2048]{2,1,0:T(8,128)S(1)}) custom-call(s32[16,12]{1,0:T(8,128)S(4)} %get-tuple-element.30.cols, bf16[16,12,128,128]{3,2,1,0:T(8,128)(2,1)S(1)} %get-tuple-element.31.tiles, bf16[16,2048]{1,0:T(8,128)(2,1)S(1)} %get-tuple-element.58.own), custom_call_target="tpu_custom_call" | custom-call | flops 100663296 | bytes 7340032 | tf_op jit(solution)/shard_map/behind/pallas_call | solution.py:198
  24.2 0.1 collective-permute-start.9
  24.3 4.2 %collective-permute-done.7.near = bf16[16,2048]{1,0:T(8,128)(2,1)S(1)} collective-permute-done((bf16[16,2048]{1,0:T(8,128)(2,1)S(1)}, bf16[16,2048]{1,0:T(8,128)(2,1)S(1)}, u32[]{:S(2)}, u32[]{:S(2)}) %collective-permute-start.7) | collective-permute-done | bytes 65568 | tf_op jit(solution)/shard_map/ppermute | solution.py:15
  28.5 0.7 %collective-permute-done.6.far = bf16[16,2048]{1,0:T(8,128)(2,1)S(1)} collective-permute-done((bf16[16,2048]{1,0:T(8,128)(2,1)S(1)}, bf16[16,2048]{1,0:T(8,128)(2,1)S(1)}, u32[]{:S(2)}, u32[]{:S(2)}) %collective-permute-start.6) | collective-permute-done | bytes 65568 | tf_op jit(solution)/shard_map/ppermute | solution.py:15
  29.2 0.1 collective-permute-start.8
  29.4 0.9 %collective-permute-start.11 = (bf16[16,2048]{1,0:T(8,128)(2,1)S(1)}, bf16[16,2048]{1,0:T(8,128)(2,1)S(1)}, u32[]{:S(2)}, u32[]{:S(2)}) collective-permute-start(bf16[16,2048]{1,0:T(8,128)(2,1)S(1)} %get-tuple-element.64), channel_id=1, source_target_pairs={{0,28},{1,29},{2,30},{3,31},{4,0},{5,1},{6,2},{7,3},{8,4},{9,5},{1... | collective-permute-start | bytes 196616 | tf_op jit(solution)/shard_map/ppermute | solution.py:15
  30.3 1.0 %collective-permute-start.10 = (bf16[16,2048]{1,0:T(8,128)(2,1)S(1)}, bf16[16,2048]{1,0:T(8,128)(2,1)S(1)}, u32[]{:S(2)}, u32[]{:S(2)}) collective-permute-start(bf16[16,2048]{1,0:T(8,128)(2,1)S(1)} %get-tuple-element.65), channel_id=1, source_target_pairs={{0,30},{1,31},{2,0},{3,1},{4,2},{5,3},{6,4},{7,5},{8,6},{9,7},{10,... | collective-permute-start | bytes 196616 | tf_op jit(solution)/shard_map/ppermute | solution.py:15
  31.3 1.8 %forward.3 = f32[16,2048]{1,0:T(8,128)S(1)} custom-call(s32[16,12]{1,0:T(8,128)S(4)} %get-tuple-element.30.cols, bf16[16,12,128,128]{3,2,1,0:T(8,128)(2,1)S(1)} %get-tuple-element.31.tiles, bf16[16,2048]{1,0:T(8,128)(2,1)S(1)} %get-tuple-element.58.own, bf16[16,2048]{1,0:T(8,128)(2,1)S(1)} %collective-permute-done.7.near, ...), custom_call_target="tpu_custom_call" | custom-call | flops 100663296 | bytes 7340032 | tf_op jit(solution)/shard_map/forward/pallas_call | solution.py:212
  33.1 0.8 %collective-permute-done.11 = bf16[16,2048]{1,0:T(8,128)(2,1)S(1)} collective-permute-done((bf16[16,2048]{1,0:T(8,128)(2,1)S(1)}, bf16[16,2048]{1,0:T(8,128)(2,1)S(1)}, u32[]{:S(2)}, u32[]{:S(2)}) %collective-permute-start.11) | collective-permute-done | bytes 65568 | tf_op jit(solution)/shard_map/ppermute | solution.py:15
  33.9 0.7 %collective-permute-done.10 = bf16[16,2048]{1,0:T(8,128)(2,1)S(1)} collective-permute-done((bf16[16,2048]{1,0:T(8,128)(2,1)S(1)}, bf16[16,2048]{1,0:T(8,128)(2,1)S(1)}, u32[]{:S(2)}, u32[]{:S(2)}) %collective-permute-start.10) | collective-permute-done | bytes 65568 | tf_op jit(solution)/shard_map/ppermute | solution.py:15
  34.6 0.7 %convert_subtract_fusion = f32[16,2048]{1,0:T(8,128)} fusion(bf16[16,2048]{1,0:T(8,128)(2,1)S(1)} %get-tuple-element.32.own, f32[16,2048]{1,0:T(8,128)S(1)} %broadcast_in_dim.27, f32[16,2048]{1,0:T(8,128)S(1)} %forward.3, pred[16,2048]{1,0:T(8,128)(4,1)S(1)} %get-tuple-element.61, f32[2,16,2048]{2,1,0:T(8,128)S(1)} %collective-permute-done.9, ...), kind=kLoop, calls=%fused_computation.4 | loop fusion | flops 425984 | bytes 1146880 | tf_op jit(solution)/shard_map/sub | solution.py:279
  (17 shorter events, 0.2 us)
Async XLA Ops:
  0.6 10.4 %collective-permute-start.1 = (bf16[16,2048]{1,0:T(8,128)(2,1)}, bf16[16,2048]{1,0:T(8,128)(2,1)S(1)}, u32[]{:S(2)}, u32[]{:S(2)}) collective-permute-start(bf16[16,2048]{1,0:T(8,128)(2,1)} %own_far.1), channel_id=1, source_target_pairs={{0,2},{1,3},{2,4},{3,5},{4,6},{5,7},{6,8},{7,9},{8,10},{9,11},{10,... | collective-permute-start | bytes 196616 | tf_op jit(solution)/shard_map/ppermute | solution.py:15
  3.6 7.7 %collective-permute-start = (bf16[16,2048]{1,0:T(8,128)(2,1)}, bf16[16,2048]{1,0:T(8,128)(2,1)S(1)}, u32[]{:S(2)}, u32[]{:S(2)}) collective-permute-start(bf16[16,2048]{1,0:T(8,128)(2,1)} %own_far.1), channel_id=1, source_target_pairs={{0,4},{1,5},{2,6},{3,7},{4,8},{5,9},{6,10},{7,11},{8,12},{9,13},{1... | collective-permute-start | bytes 196616 | tf_op jit(solution)/shard_map/ppermute | solution.py:15
  11.3 1.5 %collective-permute-start.3 = (f32[2,16,2048]{2,1,0:T(8,128)S(1)}, f32[2,16,2048]{2,1,0:T(8,128)S(1)}, u32[]{:S(2)}, u32[]{:S(2)}) collective-permute-start(f32[2,16,2048]{2,1,0:T(8,128)S(1)} %get-tuple-element.43), channel_id=1, source_target_pairs={{0,1},{1,0},{2,3},{3,2},{4,5},{5,4},{6,7},{7,6},{8,9},{9,8},{10,11... | collective-permute-start | bytes 786440 | tf_op jit(solution)/shard_map/ppermute | solution.py:19
  11.4 6.9 %collective-permute-start.2 = (bf16[2,16,2048]{2,1,0:T(8,128)(2,1)S(1)}, bf16[2,16,2048]{2,1,0:T(8,128)(2,1)S(1)}, u32[]{:S(2)}, u32[]{:S(2)}) collective-permute-start(bf16[2,16,2048]{2,1,0:T(8,128)(2,1)S(1)} %pad_maximum_fusion), channel_id=1, source_target_pairs={{0,1},{1,0},{2,3},{3,2},{4,5},{5,4},{6,7},{7,6},{8,9},{9,8},{10,11... | collective-permute-start | bytes 393224 | tf_op jit(solution)/shard_map/ppermute | solution.py:19
  13.2 6.9 %collective-permute-start.5 = (f16[16,2176]{1,0:T(8,128)(2,1)S(1)}, f16[16,2176]{1,0:T(8,128)(2,1)S(1)}, u32[]{:S(2)}, u32[]{:S(2)}) collective-permute-start(f16[16,2176]{1,0:T(8,128)(2,1)S(1)} %get-tuple-element.62), channel_id=1, source_target_pairs={{0,28},{1,29},{2,30},{3,31},{4,0},{5,1},{6,2},{7,3},{8,4},{9,5},{1... | collective-permute-start | bytes 208904 | tf_op jit(solution)/shard_map/ppermute | solution.py:15
  15.1 5.0 %collective-permute-start.4 = (f16[16,2176]{1,0:T(8,128)(2,1)S(1)}, f16[16,2176]{1,0:T(8,128)(2,1)S(1)}, u32[]{:S(2)}, u32[]{:S(2)}) collective-permute-start(f16[16,2176]{1,0:T(8,128)(2,1)S(1)} %get-tuple-element.63), channel_id=1, source_target_pairs={{0,30},{1,31},{2,0},{3,1},{4,2},{5,3},{6,4},{7,5},{8,6},{9,7},{10,... | collective-permute-start | bytes 208904 | tf_op jit(solution)/shard_map/ppermute | solution.py:15
  20.4 14.2 %copy-start = (f32[16,2048]{1,0:T(8,128)}, f32[16,2048]{1,0:T(8,128)S(1)}, u32[]{:S(2)}) copy-start(f32[16,2048]{1,0:T(8,128)S(1)} %get-tuple-element.59) | copy-start | bytes 393220
  20.4 8.1 %collective-permute-start.7 = (bf16[16,2048]{1,0:T(8,128)(2,1)S(1)}, bf16[16,2048]{1,0:T(8,128)(2,1)S(1)}, u32[]{:S(2)}, u32[]{:S(2)}) collective-permute-start(bf16[16,2048]{1,0:T(8,128)(2,1)S(1)} %get-tuple-element.58.own), channel_id=1, source_target_pairs={{0,2},{1,3},{2,4},{3,5},{4,6},{5,7},{6,8},{7,9},{8,10},{9,11},{10,... | collective-permute-start | bytes 196616 | tf_op jit(solution)/shard_map/ppermute | solution.py:15
  22.1 7.0 %collective-permute-start.6 = (bf16[16,2048]{1,0:T(8,128)(2,1)S(1)}, bf16[16,2048]{1,0:T(8,128)(2,1)S(1)}, u32[]{:S(2)}, u32[]{:S(2)}) collective-permute-start(bf16[16,2048]{1,0:T(8,128)(2,1)S(1)} %get-tuple-element.58.own), channel_id=1, source_target_pairs={{0,4},{1,5},{2,6},{3,7},{4,8},{5,9},{6,10},{7,11},{8,12},{9,13},{1... | collective-permute-start | bytes 196616 | tf_op jit(solution)/shard_map/ppermute | solution.py:15
  24.2 5.1 %collective-permute-start.9 = (f32[2,16,2048]{2,1,0:T(8,128)S(1)}, f32[2,16,2048]{2,1,0:T(8,128)S(1)}, u32[]{:S(2)}, u32[]{:S(2)}) collective-permute-start(f32[2,16,2048]{2,1,0:T(8,128)S(1)} %get-tuple-element.52), channel_id=1, source_target_pairs={{0,1},{1,0},{2,3},{3,2},{4,5},{5,4},{6,7},{7,6},{8,9},{9,8},{10,11... | collective-permute-start | bytes 786440 | tf_op jit(solution)/shard_map/ppermute | solution.py:19
  29.2 2.1 %collective-permute-start.8 = (bf16[2,16,2048]{2,1,0:T(8,128)(2,1)S(1)}, bf16[2,16,2048]{2,1,0:T(8,128)(2,1)S(1)}, u32[]{:S(2)}, u32[]{:S(2)}) collective-permute-start(bf16[2,16,2048]{2,1,0:T(8,128)(2,1)S(1)} %pad_maximum_fusion.1), channel_id=1, source_target_pairs={{0,1},{1,0},{2,3},{3,2},{4,5},{5,4},{6,7},{7,6},{8,9},{9,8},{10,11... | collective-permute-start | bytes 393224 | tf_op jit(solution)/shard_map/ppermute | solution.py:19
  29.4 4.5 %collective-permute-start.11 = (bf16[16,2048]{1,0:T(8,128)(2,1)S(1)}, bf16[16,2048]{1,0:T(8,128)(2,1)S(1)}, u32[]{:S(2)}, u32[]{:S(2)}) collective-permute-start(bf16[16,2048]{1,0:T(8,128)(2,1)S(1)} %get-tuple-element.64), channel_id=1, source_target_pairs={{0,28},{1,29},{2,30},{3,31},{4,0},{5,1},{6,2},{7,3},{8,4},{9,5},{1... | collective-permute-start | bytes 196616 | tf_op jit(solution)/shard_map/ppermute | solution.py:15
  30.3 4.3 %collective-permute-start.10 = (bf16[16,2048]{1,0:T(8,128)(2,1)S(1)}, bf16[16,2048]{1,0:T(8,128)(2,1)S(1)}, u32[]{:S(2)}, u32[]{:S(2)}) collective-permute-start(bf16[16,2048]{1,0:T(8,128)(2,1)S(1)} %get-tuple-element.65), channel_id=1, source_target_pairs={{0,30},{1,31},{2,0},{3,1},{4,2},{5,3},{6,4},{7,5},{8,6},{9,7},{10,... | collective-permute-start | bytes 196616 | tf_op jit(solution)/shard_map/ppermute | solution.py:15
